TPU v7x, 128 devices: a whole 4x4x4 slice. The times are simulated.
128 devices in a mesh: gx: 4 (over y), gy: 4 (over x), gz: 8 (over z, core).
Axes of the slice: x: 4, y: 4, z: 4, core: 2. Of those that a mesh axis runs over, the one named last changes fastest.
Arguments:
- image: float32 [64, 256, 1024], P('gx', 'gy', 'gz'), may hold values from 0 to 1
- labels: int32 [64, 256, 1024], P('gx', 'gy', 'gz'), may hold values from 0 to 2, as said below
Outputs:
- potential: float32 [64, 256, 1024], P('gx', 'gy', 'gz')
Inputs may be any that keep to these rules, and one draw needn't show every extreme that they name: `labels`: 0 marks a background seed, 1 a foreground seed, 2 an unlabeled voxel.
All inputs are finite; a program needn't handle non-finite values.
Results may differ from a plain program's by a relative error of at most 0.0001.
Values sent between devices are 32-bit elements; how exact they have to be, the bound alone decides.
A program may use at most 128 MiB of HBM per device.

v0:
```python
import jax
import jax.numpy as jnp
from jax import lax
from jax.sharding import PartitionSpec as P

SMOOTH_STEPS = 3
COARSE_STEPS = 6


HEAT_CONSTANT = 0.25
CONTRAST = 0.5
SCREENING = 0.002
SEED_WEIGHT = 1.0
THETA = 1.1
DELTA = 0.9


def extended(block, sides, width):
    for axis, dim in sides:
        count = lax.axis_size(axis)
        forward = [(i, i + 1) for i in range(count - 1)]
        backward = [(target, source) for source, target in forward]
        low = lax.ppermute(
            lax.slice_in_dim(block, block.shape[dim] - width, None, axis=dim), axis, forward
        )
        high = lax.ppermute(lax.slice_in_dim(block, 0, width, axis=dim), axis, backward)
        block = jnp.concatenate([low, block, high], axis=dim)
    return block


def soft_gradient(padded):
    central_voxel = padded[1:-1, 1:-1, 1:-1]
    beside_all = [
        padded[:-2, 1:-1, 1:-1],
        padded[2:, 1:-1, 1:-1],
        padded[1:-1, :-2, 1:-1],
        padded[1:-1, 2:, 1:-1],
        padded[1:-1, 1:-1, :-2],
        padded[1:-1, 1:-1, 2:],
    ]
    expand_region = jnp.exp(central_voxel / HEAT_CONSTANT)
    contract_region = jnp.exp(-central_voxel / HEAT_CONSTANT)
    for remaining_part in beside_all:
        expand_region = expand_region + jnp.exp(remaining_part / HEAT_CONSTANT)
        contract_region = contract_region + jnp.exp(-remaining_part / HEAT_CONSTANT)
    return HEAT_CONSTANT * jnp.log(expand_region) + HEAT_CONSTANT * jnp.log(contract_region)


def face_weights(grad):
    medium_level = grad[1:-1, 1:-1, 1:-1]
    return (
        jnp.exp(-CONTRAST * (medium_level + grad[:-2, 1:-1, 1:-1])),
        jnp.exp(-CONTRAST * (medium_level + grad[2:, 1:-1, 1:-1])),
        jnp.exp(-CONTRAST * (medium_level + grad[1:-1, :-2, 1:-1])),
        jnp.exp(-CONTRAST * (medium_level + grad[1:-1, 2:, 1:-1])),
        jnp.exp(-CONTRAST * (medium_level + grad[1:-1, 1:-1, :-2])),
        jnp.exp(-CONTRAST * (medium_level + grad[1:-1, 1:-1, 2:])),
    )


def pair_sum(arr, dims):
    for axis_dim in dims:
        shape = arr.shape
        arr = arr.reshape(shape[:axis_dim] + (shape[axis_dim] // 2, 2) + shape[axis_dim + 1 :]).sum(
            axis_dim + 1
        )
    return arr


def restrict_cells(arr):
    return pair_sum(arr, (0, 1, 2))


def coarsen_face_weights(faces):
    result = []
    for axis_dim in range(3):
        others = tuple((d for d in range(3) if d != axis_dim))
        for start in range(2):
            arr = faces[2 * axis_dim + start]
            picked = lax.slice_in_dim(arr, start, arr.shape[axis_dim], 2, axis_dim)
            result.append(pair_sum(picked, others))
    return tuple(result)


def prolong(arr):
    return jnp.repeat(jnp.repeat(jnp.repeat(arr, 2, 0), 2, 1), 2, 2)


def diagonal(cells, faces):
    total = cells
    for face in faces:
        total = total + face
    return total


def apply_operator(field, padded, diag, faces):
    return diag * field - (
        faces[0] * padded[:-2, 1:-1, 1:-1]
        + faces[1] * padded[2:, 1:-1, 1:-1]
        + faces[2] * padded[1:-1, :-2, 1:-1]
        + faces[3] * padded[1:-1, 2:, 1:-1]
        + faces[4] * padded[1:-1, 1:-1, :-2]
        + faces[5] * padded[1:-1, 1:-1, 2:]
    )


def chebyshev(operate, inverse, rhs, field, steps, inside=None):
    sigma = THETA / DELTA
    if field is None:
        resid = rhs
        field = jnp.zeros_like(rhs)
    else:
        resid = rhs - operate(field)
    update = inverse * resid / THETA
    field = field + update
    rho = 1.0 / sigma
    for step in range(steps - 1):
        resid = rhs - operate(field)
        rho_new = 1.0 / (2.0 * sigma - rho)
        update = rho_new * rho * update + 2.0 * rho_new / DELTA * inverse * resid
        field = field + update
        rho = rho_new
    return field


def pad_fine(field):
    return extended(field, (("gx", 0), ("gy", 1), ("gz", 2)), 1)


def padded_medium_collected(field):
    padded = extended(field, (("gy", 1), ("gz", 2)), 1)
    return jnp.pad(padded, ((1, 1), (0, 0), (0, 0)))


def pad_low_gathered(field):
    padded = extended(field, (("gz", 2),), 1)
    return jnp.pad(padded, ((1, 1), (1, 1), (0, 0)))


def make_operator(pad_fn, diag, faces):

    def operate(field):
        return apply_operator(field, pad_fn(field), diag, faces)

    return operate


def shards(image, labels):
    rows_x, rows_y = (image.shape[0], image.shape[1])
    depth = 0
    padded_image = extended(image, (("gx", 0), ("gy", 1), ("gz", 2)), 2 + depth)
    faces_wide = face_weights(soft_gradient(padded_image))
    cells = SCREENING + SEED_WEIGHT * (labels != 2).astype(jnp.float32)
    rhs = SEED_WEIGHT * (labels == 1).astype(jnp.float32)
    diag = diagonal(cells, faces_wide)
    fine_op = make_operator(pad_fine, diag, faces_wide)
    field = chebyshev(fine_op, 1.0 / diag, rhs, None, SMOOTH_STEPS)
    resid_fine = rhs - fine_op(field)
    resid_mid = restrict_cells(resid_fine)
    cells_mid = restrict_cells(cells)
    faces_mid = coarsen_face_weights(faces_wide)
    moved = (
        lax.all_gather(resid_mid, "gx", axis=0, tiled=True),
        lax.all_gather(cells_mid, "gx", axis=0, tiled=True),
        lax.all_gather(faces_mid[0], "gx", axis=0, tiled=True),
        lax.all_gather(faces_mid[1], "gx", axis=0, tiled=True),
        lax.all_gather(faces_mid[2], "gx", axis=0, tiled=True),
        lax.all_gather(faces_mid[3], "gx", axis=0, tiled=True),
        lax.all_gather(faces_mid[4], "gx", axis=0, tiled=True),
        lax.all_gather(faces_mid[5], "gx", axis=0, tiled=True),
    )
    resid_mid, cells_mid, faces_mid = (moved[0], moved[1], tuple(moved[2:]))
    diag_mid = diagonal(cells_mid, faces_mid)
    mid_op = make_operator(padded_medium_collected, diag_mid, faces_mid)
    corr_mid = chebyshev(mid_op, 1.0 / diag_mid, resid_mid, None, SMOOTH_STEPS)
    resid_low = restrict_cells(resid_mid - mid_op(corr_mid))
    cells_low = restrict_cells(cells_mid)
    faces_low = coarsen_face_weights(faces_mid)
    moved_low = (
        lax.all_gather(resid_low, "gy", axis=1, tiled=True),
        lax.all_gather(cells_low, "gy", axis=1, tiled=True),
        lax.all_gather(faces_low[0], "gy", axis=1, tiled=True),
        lax.all_gather(faces_low[1], "gy", axis=1, tiled=True),
        lax.all_gather(faces_low[2], "gy", axis=1, tiled=True),
        lax.all_gather(faces_low[3], "gy", axis=1, tiled=True),
        lax.all_gather(faces_low[4], "gy", axis=1, tiled=True),
        lax.all_gather(faces_low[5], "gy", axis=1, tiled=True),
    )
    resid_low, cells_low, faces_low = (moved_low[0], moved_low[1], tuple(moved_low[2:]))
    diag_low = diagonal(cells_low, faces_low)
    low_op = make_operator(pad_low_gathered, diag_low, faces_low)
    corr_low = chebyshev(low_op, 1.0 / diag_low, resid_low, None, COARSE_STEPS)
    quarter_y = rows_y // 4
    own_low = lax.dynamic_slice_in_dim(corr_low, lax.axis_index("gy") * quarter_y, quarter_y, 1)
    corr_mid = chebyshev(
        mid_op, 1.0 / diag_mid, resid_mid, corr_mid + prolong(own_low), SMOOTH_STEPS
    )
    half_x = rows_x // 2
    corr_mid = lax.dynamic_slice_in_dim(corr_mid, lax.axis_index("gx") * half_x, half_x, 0)
    start = field + prolong(corr_mid)
    return chebyshev(fine_op, 1.0 / diag, rhs, start, SMOOTH_STEPS)


def solution(mesh):
    placed = (P("gx", "gy", "gz"), P("gx", "gy", "gz"))
    return jax.shard_map(
        shards, mesh=mesh, in_specs=placed, out_specs=P("gx", "gy", "gz"), check_vma=False
    )
```

profile of v0, /device:TPU:0, one launch (start us, length us, event | category | flops | bytes accessed | tf_op | source)
XLA Modules:
  0.0 888.9 jit_solution(11454077383671735675)
XLA Ops:
  40.8 15.1 %all_gather.51 = f32[32,32,64]{1,0,2:T(8,128)S(1)} all-gather(f32[8,32,64]{1,0,2:T(8,128)S(1)} %bitcast_reduce_fusion.8), channel_id=1, replica_groups=mesh['gx'=4,'gy'=4,'gz'=8] {'gx'}, dimensions={0}, use_global_device_ids=true | all-gather | bytes 327680 | tf_op jit(solution)/shard_map/all_gather | solution.py:167
  66.3 15.4 %all_gather.52 = f32[32,32,64]{1,0,2:T(8,128)S(1)} all-gather(f32[8,32,64]{1,0,2:T(8,128)S(1)} %bitcast_reduce_fusion.7), channel_id=1, replica_groups=mesh['gx'=4,'gy'=4,'gz'=8] {'gx'}, dimensions={0}, use_global_device_ids=true | all-gather | bytes 327680 | tf_op jit(solution)/shard_map/all_gather | solution.py:168
  92.3 14.2 %all_gather.49 = f32[32,32,64]{1,0,2:T(8,128)S(1)} all-gather(f32[8,32,64]{1,0,2:T(8,128)S(1)} %bitcast_reduce_fusion.10), channel_id=1, replica_groups=mesh['gx'=4,'gy'=4,'gz'=8] {'gx'}, dimensions={0}, use_global_device_ids=true | all-gather | bytes 327680 | tf_op jit(solution)/shard_map/all_gather | solution.py:165
  116.7 15.2 %all_gather.50 = f32[32,32,64]{1,0,2:T(8,128)S(1)} all-gather(f32[8,32,64]{1,0,2:T(8,128)S(1)} %bitcast_reduce_fusion.9), channel_id=1, replica_groups=mesh['gx'=4,'gy'=4,'gz'=8] {'gx'}, dimensions={0}, use_global_device_ids=true | all-gather | bytes 327680 | tf_op jit(solution)/shard_map/all_gather | solution.py:166
  141.8 13.8 %all_gather.48 = f32[32,32,64]{1,0,2:T(8,128)S(1)} all-gather(f32[8,32,64]{1,0,2:T(8,128)S(1)} %bitcast_reduce_fusion.11), channel_id=1, replica_groups=mesh['gx'=4,'gy'=4,'gz'=8] {'gx'}, dimensions={0}, use_global_device_ids=true | all-gather | bytes 327680 | tf_op jit(solution)/shard_map/all_gather | solution.py:164
  168.4 11.2 %slice.778 = f32[16,64,64]{2,0,1:T(8,128)} slice(f32[16,64,128]{2,0,1:T(8,128)S(1)} %copy-done.49), slice={[0:16:1], [0:64:1], [0:128:2]} | slice | bytes 524288 | tf_op jit(solution)/shard_map/slice | solution.py:80
  202.1 17.0 %all_gather.53 = f32[32,32,64]{1,0,2:T(8,128)S(1)} all-gather(f32[8,32,64]{1,0,2:T(8,128)S(1)} %copy-done.95), channel_id=1, replica_groups=mesh['gx'=4,'gy'=4,'gz'=8] {'gx'}, dimensions={0}, use_global_device_ids=true | all-gather | bytes 327680 | tf_op jit(solution)/shard_map/all_gather | solution.py:169
  241.8 11.3 %slice.779 = f32[16,64,64]{2,0,1:T(8,128)} slice(f32[16,64,128]{2,0,1:T(8,128)S(1)} %copy-done.51), slice={[0:16:1], [0:64:1], [1:128:2]} | slice | bytes 524288 | tf_op jit(solution)/shard_map/slice | solution.py:80
  272.6 15.5 %all_gather.54 = f32[32,32,64]{1,0,2:T(8,128)S(1)} all-gather(f32[8,32,64]{1,0,2:T(8,128)} %copy.106), channel_id=1, replica_groups=mesh['gx'=4,'gy'=4,'gz'=8] {'gx'}, dimensions={0}, use_global_device_ids=true | all-gather | bytes 327680 | tf_op jit(solution)/shard_map/all_gather | solution.py:170
  321.0 14.7 %all_gather.59 = f32[16,64,32]{2,0,1:T(8,128)} all-gather(f32[16,16,32]{2,0,1:T(8,128)} %copy.135), channel_id=1, replica_groups=mesh['gx'=4,'gy'=4,'gz'=8] {'gy'}, dimensions={1}, use_global_device_ids=true | all-gather | bytes 163840 | tf_op jit(solution)/shard_map/all_gather | solution.py:184
  347.4 13.9 %all_gather.60 = f32[16,64,32]{2,0,1:T(8,128)} all-gather(f32[16,16,32]{2,0,1:T(8,128)} %copy.138), channel_id=1, replica_groups=mesh['gx'=4,'gy'=4,'gz'=8] {'gy'}, dimensions={1}, use_global_device_ids=true | all-gather | bytes 163840 | tf_op jit(solution)/shard_map/all_gather | solution.py:185
  380.2 14.3 %all_gather.55 = f32[32,32,64]{1,0,2:T(8,128)S(1)} all-gather(f32[8,32,64]{1,0,2:T(8,128)S(1)} %bitcast_reduce_fusion.6), channel_id=1, replica_groups=mesh['gx'=4,'gy'=4,'gz'=8] {'gx'}, dimensions={0}, use_global_device_ids=true | all-gather | bytes 327680 | tf_op jit(solution)/shard_map/all_gather | solution.py:163
  408.5 15.9 %all_gather.57 = f32[16,64,32]{2,0,1:T(8,128)} all-gather(f32[16,16,32]{2,0,1:T(8,128)} %copy.129), channel_id=1, replica_groups=mesh['gx'=4,'gy'=4,'gz'=8] {'gy'}, dimensions={1}, use_global_device_ids=true | all-gather | bytes 163840 | tf_op jit(solution)/shard_map/all_gather | solution.py:182
  436.4 13.7 %all_gather.58 = f32[16,64,32]{2,0,1:T(8,128)} all-gather(f32[16,16,32]{2,0,1:T(8,128)} %copy.132), channel_id=1, replica_groups=mesh['gx'=4,'gy'=4,'gz'=8] {'gy'}, dimensions={1}, use_global_device_ids=true | all-gather | bytes 163840 | tf_op jit(solution)/shard_map/all_gather | solution.py:183
  466.7 16.2 %all_gather.61 = f32[16,64,32]{2,0,1:T(8,128)} all-gather(f32[16,16,32]{2,0,1:T(8,128)} %bitcast_reduce_fusion.14), channel_id=1, replica_groups=mesh['gx'=4,'gy'=4,'gz'=8] {'gy'}, dimensions={1}, use_global_device_ids=true | all-gather | bytes 163840 | tf_op jit(solution)/shard_map/all_gather | solution.py:186
  498.0 14.2 %all_gather.62 = f32[16,64,32]{2,0,1:T(8,128)} all-gather(f32[16,16,32]{2,0,1:T(8,128)S(1)} %copy-done.98), channel_id=1, replica_groups=mesh['gx'=4,'gy'=4,'gz'=8] {'gy'}, dimensions={1}, use_global_device_ids=true | all-gather | bytes 163840 | tf_op jit(solution)/shard_map/all_gather | solution.py:187
  515.9 8.0 fusion.51
  531.8 16.0 %all_gather.56 = f32[16,64,32]{2,0,1:T(8,128)} all-gather(f32[16,16,32]{2,0,1:T(8,128)S(1)} %copy-done.99), channel_id=1, replica_groups=mesh['gx'=4,'gy'=4,'gz'=8] {'gy'}, dimensions={1}, use_global_device_ids=true | all-gather | bytes 163840 | tf_op jit(solution)/shard_map/all_gather | solution.py:181
  568.7 7.2 fusion.37
  585.2 14.0 %all_gather.63 = f32[16,64,32]{2,0,1:T(8,128)S(1)} all-gather(f32[16,16,32]{2,0,1:T(8,128)} %copy.149), channel_id=1, replica_groups=mesh['gx'=4,'gy'=4,'gz'=8] {'gy'}, dimensions={1}, use_global_device_ids=true | all-gather | bytes 163840 | tf_op jit(solution)/shard_map/all_gather | solution.py:180
  612.3 9.1 %collective-permute-start.38 = (f32[16,64,1]{2,0,1:T(8,128)S(1)}, f32[16,64,1]{2,0,1:T(8,128)S(1)}, u32[]{:S(2)}, u32[]{:S(2)}) collective-permute-start(f32[16,64,1]{2,0,1:T(8,128)S(1)} %get-tuple-element.99), channel_id=1, source_target_pairs={{0,1},{1,2},{2,3},{3,4},{4,5},{5,6},{6,7},{8,9},{9,10},{10,11},{11... | collective-permute-start | bytes 12296 | tf_op jit(solution)/shard_map/ppermute | solution.py:23
  626.9 8.6 collective-permute-start.40
  642.1 8.6 collective-permute-start.42
  660.8 9.4 %collective-permute-start.44 = (f32[16,64,1]{2,0,1:T(8,128)}, f32[16,64,1]{2,0,1:T(8,128)}, u32[]{:S(2)}, u32[]{:S(2)}) collective-permute-start(f32[16,64,1]{2,0,1:T(8,128)} %get-tuple-element.93), channel_id=1, source_target_pairs={{0,1},{1,2},{2,3},{3,4},{4,5},{5,6},{6,7},{8,9},{9,10},{10,11},{11... | collective-permute-start | bytes 12296 | tf_op jit(solution)/shard_map/ppermute | solution.py:23
  (566 shorter events, 573.7 us)
Async XLA Ops:
  163.8 18.2 %collective-permute-start.6 = (f32[1,64,128]{2,0,1:T(1,128)}, f32[1,64,128]{2,0,1:T(1,128)}, u32[]{:S(2)}, u32[]{:S(2)}) collective-permute-start(f32[1,64,128]{2,0,1:T(1,128)} %get-tuple-element.108), channel_id=1, source_target_pairs={{0,32},{32,64},{64,96},{1,33},{33,65},{65,97},{2,34},{34,66},{66,9... | collective-permute-start | bytes 98312 | tf_op jit(solution)/shard_map/ppermute | solution.py:23
  166.0 16.0 %collective-permute-start.7 = (f32[1,64,128]{2,0,1:T(1,128)}, f32[1,64,128]{2,0,1:T(1,128)}, u32[]{:S(2)}, u32[]{:S(2)}) collective-permute-start(f32[1,64,128]{2,0,1:T(1,128)} %get-tuple-element.109), channel_id=1, source_target_pairs={{32,0},{64,32},{96,64},{33,1},{65,33},{97,65},{34,2},{66,34},{98,6... | collective-permute-start | bytes 98312 | tf_op jit(solution)/shard_map/ppermute | solution.py:26
  197.0 28.3 %collective-permute-start.10 = (f32[18,66,1]{1,2,0:T(1,128)}, f32[18,66,1]{1,2,0:T(1,128)}, u32[]{:S(2)}, u32[]{:S(2)}) collective-permute-start(f32[18,66,1]{1,2,0:T(1,128)} %copy.92), channel_id=1, source_target_pairs={{0,1},{1,2},{2,3},{3,4},{4,5},{5,6},{6,7},{8,9},{9,10},{10,11},{11... | collective-permute-start | bytes 14264 | tf_op jit(solution)/shard_map/ppermute | solution.py:23
  200.8 26.4 %collective-permute-start.11 = (f32[18,66,1]{1,2,0:T(1,128)}, f32[18,66,1]{1,2,0:T(1,128)}, u32[]{:S(2)}, u32[]{:S(2)}) collective-permute-start(f32[18,66,1]{1,2,0:T(1,128)} %copy.94), channel_id=1, source_target_pairs={{1,0},{2,1},{3,2},{4,3},{5,4},{6,5},{7,6},{9,8},{10,9},{11,10},{12... | collective-permute-start | bytes 14264 | tf_op jit(solution)/shard_map/ppermute | solution.py:26
  236.6 18.1 %collective-permute-start.12 = (f32[1,64,128]{2,0,1:T(1,128)}, f32[1,64,128]{2,0,1:T(1,128)}, u32[]{:S(2)}, u32[]{:S(2)}) collective-permute-start(f32[1,64,128]{2,0,1:T(1,128)} %get-tuple-element.106), channel_id=1, source_target_pairs={{0,32},{32,64},{64,96},{1,33},{33,65},{65,97},{2,34},{34,66},{66,9... | collective-permute-start | bytes 98312 | tf_op jit(solution)/shard_map/ppermute | solution.py:23
  239.8 14.9 %collective-permute-start.13 = (f32[1,64,128]{2,0,1:T(1,128)}, f32[1,64,128]{2,0,1:T(1,128)}, u32[]{:S(2)}, u32[]{:S(2)}) collective-permute-start(f32[1,64,128]{2,0,1:T(1,128)} %get-tuple-element.107), channel_id=1, source_target_pairs={{32,0},{64,32},{96,64},{33,1},{65,33},{97,65},{34,2},{66,34},{98,6... | collective-permute-start | bytes 98312 | tf_op jit(solution)/shard_map/ppermute | solution.py:26
  268.4 24.8 %collective-permute-start.16 = (f32[18,66,1]{1,2,0:T(1,128)}, f32[18,66,1]{1,2,0:T(1,128)}, u32[]{:S(2)}, u32[]{:S(2)}) collective-permute-start(f32[18,66,1]{1,2,0:T(1,128)} %copy.96), channel_id=1, source_target_pairs={{0,1},{1,2},{2,3},{3,4},{4,5},{5,6},{6,7},{8,9},{9,10},{10,11},{11... | collective-permute-start | bytes 14264 | tf_op jit(solution)/shard_map/ppermute | solution.py:23
  271.3 23.9 %collective-permute-start.17 = (f32[18,66,1]{1,2,0:T(1,128)}, f32[18,66,1]{1,2,0:T(1,128)}, u32[]{:S(2)}, u32[]{:S(2)}) collective-permute-start(f32[18,66,1]{1,2,0:T(1,128)} %copy.98), channel_id=1, source_target_pairs={{1,0},{2,1},{3,2},{4,3},{5,4},{6,5},{7,6},{9,8},{10,9},{11,10},{12... | collective-permute-start | bytes 14264 | tf_op jit(solution)/shard_map/ppermute | solution.py:26
  316.6 20.9 %collective-permute-start.20 = (f32[18,1,128]{2,0,1:T(8,128)}, f32[18,1,128]{2,0,1:T(8,128)S(1)}, u32[]{:S(2)}, u32[]{:S(2)}) collective-permute-start(f32[18,1,128]{2,0,1:T(8,128)} %get-tuple-element.79), channel_id=1, source_target_pairs={{0,8},{8,16},{16,24},{1,9},{9,17},{17,25},{2,10},{10,18},{18,26},{... | collective-permute-start | bytes 27656 | tf_op jit(solution)/shard_map/ppermute | solution.py:23
  319.7 17.8 %collective-permute-start.21 = (f32[18,1,128]{2,0,1:T(8,128)}, f32[18,1,128]{2,0,1:T(8,128)}, u32[]{:S(2)}, u32[]{:S(2)}) collective-permute-start(f32[18,1,128]{2,0,1:T(8,128)} %get-tuple-element.80), channel_id=1, source_target_pairs={{8,0},{16,8},{24,16},{9,1},{17,9},{25,17},{10,2},{18,10},{26,18},{... | collective-permute-start | bytes 27656 | tf_op jit(solution)/shard_map/ppermute | solution.py:26
  342.2 20.8 %collective-permute-start.22 = (f32[18,66,1]{1,2,0:T(1,128)}, f32[18,66,1]{1,2,0:T(1,128)}, u32[]{:S(2)}, u32[]{:S(2)}) collective-permute-start(f32[18,66,1]{1,2,0:T(1,128)} %copy.107), channel_id=1, source_target_pairs={{0,1},{1,2},{2,3},{3,4},{4,5},{5,6},{6,7},{8,9},{9,10},{10,11},{11... | collective-permute-start | bytes 14264 | tf_op jit(solution)/shard_map/ppermute | solution.py:23
  346.1 18.9 %collective-permute-start.23 = (f32[18,66,1]{1,2,0:T(1,128)}, f32[18,66,1]{1,2,0:T(1,128)}, u32[]{:S(2)}, u32[]{:S(2)}) collective-permute-start(f32[18,66,1]{1,2,0:T(1,128)} %copy.109), channel_id=1, source_target_pairs={{1,0},{2,1},{3,2},{4,3},{5,4},{6,5},{7,6},{9,8},{10,9},{11,10},{12... | collective-permute-start | bytes 14264 | tf_op jit(solution)/shard_map/ppermute | solution.py:26
  402.0 24.1 %collective-permute-start.24 = (f32[32,1,64]{2,0,1:T(8,128)S(1)}, f32[32,1,64]{2,0,1:T(8,128)}, u32[]{:S(2)}, u32[]{:S(2)}) collective-permute-start(f32[32,1,64]{2,0,1:T(8,128)S(1)} %copy.112), channel_id=1, source_target_pairs={{0,8},{8,16},{16,24},{1,9},{9,17},{17,25},{2,10},{10,18},{18,26},{... | collective-permute-start | bytes 24584 | tf_op jit(solution)/shard_map/ppermute | solution.py:23
  407.2 21.4 %collective-permute-start.25 = (f32[32,1,64]{2,0,1:T(8,128)}, f32[32,1,64]{2,0,1:T(8,128)}, u32[]{:S(2)}, u32[]{:S(2)}) collective-permute-start(f32[32,1,64]{2,0,1:T(8,128)} %copy.113), channel_id=1, source_target_pairs={{8,0},{16,8},{24,16},{9,1},{17,9},{25,17},{10,2},{18,10},{26,18},{... | collective-permute-start | bytes 24584 | tf_op jit(solution)/shard_map/ppermute | solution.py:26
  432.2 18.0 %collective-permute-start.26 = (f32[32,34,1]{1,0,2:T(8,128)S(1)}, f32[32,34,1]{1,0,2:T(8,128)S(1)}, u32[]{:S(2)}, u32[]{:S(2)}) collective-permute-start(f32[32,34,1]{1,0,2:T(8,128)S(1)} %get-tuple-element.43), channel_id=1, source_target_pairs={{0,1},{1,2},{2,3},{3,4},{4,5},{5,6},{6,7},{8,9},{9,10},{10,11},{11... | collective-permute-start | bytes 13064 | tf_op jit(solution)/shard_map/ppermute | solution.py:23
  435.1 15.1 %collective-permute-start.27 = (f32[32,34,1]{1,0,2:T(8,128)S(1)}, f32[32,34,1]{1,0,2:T(8,128)S(1)}, u32[]{:S(2)}, u32[]{:S(2)}) collective-permute-start(f32[32,34,1]{1,0,2:T(8,128)S(1)} %get-tuple-element.44), channel_id=1, source_target_pairs={{1,0},{2,1},{3,2},{4,3},{5,4},{6,5},{7,6},{9,8},{10,9},{11,10},{12... | collective-permute-start | bytes 13064 | tf_op jit(solution)/shard_map/ppermute | solution.py:26
  461.3 21.7 %collective-permute-start.28 = (f32[32,1,64]{2,0,1:T(8,128)S(1)}, f32[32,1,64]{2,0,1:T(8,128)}, u32[]{:S(2)}, u32[]{:S(2)}) collective-permute-start(f32[32,1,64]{2,0,1:T(8,128)S(1)} %copy.118), channel_id=1, source_target_pairs={{0,8},{8,16},{16,24},{1,9},{9,17},{17,25},{2,10},{10,18},{18,26},{... | collective-permute-start | bytes 24584 | tf_op jit(solution)/shard_map/ppermute | solution.py:23
  465.3 20.2 %collective-permute-start.29 = (f32[32,1,64]{2,0,1:T(8,128)}, f32[32,1,64]{2,0,1:T(8,128)}, u32[]{:S(2)}, u32[]{:S(2)}) collective-permute-start(f32[32,1,64]{2,0,1:T(8,128)} %copy.119), channel_id=1, source_target_pairs={{8,0},{16,8},{24,16},{9,1},{17,9},{25,17},{10,2},{18,10},{26,18},{... | collective-permute-start | bytes 24584 | tf_op jit(solution)/shard_map/ppermute | solution.py:26
  489.6 23.5 %collective-permute-start.30 = (f32[32,34,1]{1,0,2:T(8,128)}, f32[32,34,1]{1,0,2:T(8,128)S(1)}, u32[]{:S(2)}, u32[]{:S(2)}) collective-permute-start(f32[32,34,1]{1,0,2:T(8,128)} %get-tuple-element.41), channel_id=1, source_target_pairs={{0,1},{1,2},{2,3},{3,4},{4,5},{5,6},{6,7},{8,9},{9,10},{10,11},{11... | collective-permute-start | bytes 13064 | tf_op jit(solution)/shard_map/ppermute | solution.py:23
  496.7 16.4 %collective-permute-start.31 = (f32[32,34,1]{1,0,2:T(8,128)}, f32[32,34,1]{1,0,2:T(8,128)}, u32[]{:S(2)}, u32[]{:S(2)}) collective-permute-start(f32[32,34,1]{1,0,2:T(8,128)} %get-tuple-element.42), channel_id=1, source_target_pairs={{1,0},{2,1},{3,2},{4,3},{5,4},{6,5},{7,6},{9,8},{10,9},{11,10},{12... | collective-permute-start | bytes 13064 | tf_op jit(solution)/shard_map/ppermute | solution.py:26
  527.4 20.3 %collective-permute-start.32 = (f32[32,1,64]{2,0,1:T(8,128)S(1)}, f32[32,1,64]{2,0,1:T(8,128)S(1)}, u32[]{:S(2)}, u32[]{:S(2)}) collective-permute-start(f32[32,1,64]{2,0,1:T(8,128)S(1)} %copy.141), channel_id=1, source_target_pairs={{0,8},{8,16},{16,24},{1,9},{9,17},{17,25},{2,10},{10,18},{18,26},{... | collective-permute-start | bytes 24584 | tf_op jit(solution)/shard_map/ppermute | solution.py:23
  530.5 19.1 %collective-permute-start.33 = (f32[32,1,64]{2,0,1:T(8,128)S(1)}, f32[32,1,64]{2,0,1:T(8,128)S(1)}, u32[]{:S(2)}, u32[]{:S(2)}) collective-permute-start(f32[32,1,64]{2,0,1:T(8,128)S(1)} %copy.142), channel_id=1, source_target_pairs={{8,0},{16,8},{24,16},{9,1},{17,9},{25,17},{10,2},{18,10},{26,18},{... | collective-permute-start | bytes 24584 | tf_op jit(solution)/shard_map/ppermute | solution.py:26
  612.3 10.6 %collective-permute-start.38 = (f32[16,64,1]{2,0,1:T(8,128)S(1)}, f32[16,64,1]{2,0,1:T(8,128)S(1)}, u32[]{:S(2)}, u32[]{:S(2)}) collective-permute-start(f32[16,64,1]{2,0,1:T(8,128)S(1)} %get-tuple-element.99), channel_id=1, source_target_pairs={{0,1},{1,2},{2,3},{3,4},{4,5},{5,6},{6,7},{8,9},{9,10},{10,11},{11... | collective-permute-start | bytes 12296 | tf_op jit(solution)/shard_map/ppermute | solution.py:23
  660.8 10.7 %collective-permute-start.44 = (f32[16,64,1]{2,0,1:T(8,128)}, f32[16,64,1]{2,0,1:T(8,128)}, u32[]{:S(2)}, u32[]{:S(2)}) collective-permute-start(f32[16,64,1]{2,0,1:T(8,128)} %get-tuple-element.93), channel_id=1, source_target_pairs={{0,1},{1,2},{2,3},{3,4},{4,5},{5,6},{6,7},{8,9},{9,10},{10,11},{11... | collective-permute-start | bytes 12296 | tf_op jit(solution)/shard_map/ppermute | solution.py:23
  (153 other events, 1329.5 us)
where the time goes:
time: 905 us; the launch traced here: 889 us
  blocking collectives  239 us (26%)
  local copies, waits for them, and re-layouts  198 us (22%)
  starting transfers between devices  189 us (21%)
  other arithmetic  172 us (19%)
  waiting for transfers between devices  88.5 us (10%)
    ppermute x38, starting transfers between devices, extended(): lax.ppermute(lax.slice_in_dim(block, block.shape[dim] - width, None, axis...  138 us
    ppermute x38, waiting for transfers between devices, extended(): lax.ppermute(lax.slice_in_dim(block, 0, width, axis=dim), axis, backward)  86 us
    add x15, other arithmetic, chebyshev(): field = field + update  63.8 us
    ppermute x38, starting transfers between devices, extended(): lax.ppermute(lax.slice_in_dim(block, 0, width, axis=dim), axis, backward)  50.7 us
    slice x14, local copies, waits for them, and re-layouts, coarsen_face_weights(): picked = lax.slice_in_dim(arr, start, arr.shape[axis_dim], 2, axis_dim)  46.5 us
    slice x38, local copies, waits for them, and re-layouts, extended(): lax.slice_in_dim(block, block.shape[dim] - width, None, axis=dim)  42.4 us
    reduce_sum x36, other arithmetic, pair_sum(): arr.reshape(shape[:axis_dim] + (shape[axis_dim] // 2, 2) + shape[axis_dim...  40.5 us
    ppermute x13, local copies, waits for them, and re-layouts, extended(): lax.ppermute(lax.slice_in_dim(block, 0, width, axis=dim), axis, backward)  23.5 us
  transfers between devices with their start and end apart: 76, of which 37 were waited for; matrix products, arithmetic and copies ran while one was open for 11% of the time, Pallas kernels for 0%

commit v1 on v0

v1 whole, which is shorter than its diff:
```python
import jax
import jax.numpy as jnp
from jax import lax
from jax.experimental import pallas as pl
from jax.experimental.pallas import tpu as pltpu
from jax.sharding import PartitionSpec as P

SMOOTH_STEPS = 3
COARSE_STEPS = 6
HEAT_CONSTANT = 0.25
SCREENING = 0.002
SEED_WEIGHT = 1.0
THETA = 1.1
DELTA = 0.9

MESH = pl.DeviceIdType.MESH
F32 = jnp.float32
SIZES = {"gx": 4, "gy": 4, "gz": 8}

X0, Y0 = 32, 96
X1, Y1 = 24, 64
X2, Y2 = 24, 48

PLANAR = [(dx, dy) for dx in (1, -1, 0) for dy in (1, -1, 0) if (dx, dy) != (0, 0)]
COLUMN = [(dx, dy) for dx in (1, -1, 2, 0) for dy in (1, -1, 0) if (dx, dy) != (0, 0)]


def factors(steps):
    sigma = THETA / DELTA
    rho = 1.0 / sigma
    out = []
    for _ in range(steps - 1):
        rho_new = 1.0 / (2.0 * sigma - rho)
        out.append((rho_new * rho, 2.0 * rho_new / DELTA))
        rho = rho_new
    return out


def peer(dx, dy, dz):
    shift = {"gx": dx, "gy": dy, "gz": dz}
    return {a: lax.rem(lax.axis_index(a) + shift[a] + n, n) for a, n in SIZES.items()}


def dot(a, b):
    return jnp.dot(a, b, precision=lax.Precision.HIGHEST, preferred_element_type=F32)


def kernel(
    image, labels, out,
    E, L, R, H, UA, UB, DU, C, Q, DH, M,
    zs0, zr0, tmp, bufs, wyb, c1, wx1, wy1, wz1, D1,
    L1, zs1, zr1, A1, I1, C1, ea1, eb1, d1,
    L2, zs2, zr2, A2, I2, C2, ea2, eb2, d2, D2, pro,
    s_e, r_e, s_l, r_l, s_z0, r_z0, s_b0, r_b0,
    s_a1, r_a1, s_b1, r_b1, s_a2, r_a2, s_b2, r_b2,
):
    gx, gy, gz = (lax.axis_index(a) for a in ("gx", "gy", "gz"))
    barrier = pltpu.get_barrier_semaphore()
    partners = [(dx, dy, 0) for dx, dy in COLUMN] + [(0, 0, 1), (0, 0, -1)]
    for p in partners:
        pl.semaphore_signal(barrier, inc=1, device_id=peer(*p), device_id_type=MESH)

    def lanes(rows):
        return lax.broadcasted_iota(jnp.int32, (rows, 128), 1)

    def rows_of(rows):
        return lax.broadcasted_iota(jnp.int32, (rows, 128), 0)

    def send(src, dst, ssem, rsem, to):
        copy = pltpu.make_async_remote_copy(
            src_ref=src, dst_ref=dst, send_sem=ssem, recv_sem=rsem, device_id=to, device_id_type=MESH
        )
        copy.start()
        return copy

    started = []

    def loop(lo, hi, body):
        def step(i, carry):
            body(i)
            return carry
        lax.fori_loop(lo, hi, step, 0)

    def own(x):
        E[0, 8 + x, 16:80] = jnp.exp(image[x] * (1.0 / HEAT_CONSTANT))
        L[0, 8 + x, 16:80] = labels[x].astype(F32)
    loop(0, 16, own)
    pl.semaphore_wait(barrier, len(partners))

    def x_range(dx, start, count, width):
        if dx == 0:
            return pl.ds(start, count), pl.ds(start, count)
        if dx == 1:
            return pl.ds(start + count - width, width), pl.ds(start - width, width)
        return pl.ds(start, width), pl.ds(start + count, width)

    def y_range(dy, start, count):
        if dy == 0:
            return pl.ds(start, count), pl.ds(start, count)
        if dy == 1:
            return pl.ds(start + count - 8, 8), pl.ds(start - 8, 8)
        return pl.ds(start, 8), pl.ds(start + count, 8)

    first = []
    for i, (dx, dy) in enumerate(PLANAR):
        ys, yd = y_range(dy, 16, 64)
        xs, xd = x_range(dx, 8, 16, 7)
        first.append(send(E.at[0, xs, ys], E.at[0, xd, yd], s_e.at[i], r_e.at[i], peer(dx, dy, 0)))
        xs, xd = x_range(dx, 8, 16, 5)
        first.append(send(L.at[0, xs, ys], L.at[0, xd, yd], s_l.at[i], r_l.at[i], peer(dx, dy, 0)))

    group64 = lanes(64) // 8

    def pack(p, carry):
        result = []
        for k, ref in enumerate((E, L)):
            v = ref[0, 8 + p, 16:80]
            low = pltpu.roll(v, lax.rem(8 * p, 128), 1)
            high = pltpu.roll(v, lax.rem(8 * p + 8, 128), 1)
            result.append(jnp.where(group64 == p, low, carry[2 * k]))
            result.append(jnp.where(group64 == p, high, carry[2 * k + 1]))
        return tuple(result)

    zero64 = jnp.zeros((64, 128), F32)
    packed = lax.fori_loop(0, 16, pack, (zero64,) * 4)
    for k in range(2):
        zs0[1, k] = packed[2 * k]
        zs0[0, k] = packed[2 * k + 1]
    za = [
        send(zs0.at[s], zr0.at[1, s, :, pl.ds(8, 64)], s_z0.at[s], r_z0.at[s], peer(0, 0, 1 if s == 0 else -1))
        for s in range(2)
    ]

    for ref in (ea1, eb1, d1):
        def clear(x, ref=ref):
            ref[x] = jnp.zeros((Y1, 128), F32)
        loop(0, X1, clear)
    for ref in (ea2, eb2, d2):
        def clear(x, ref=ref):
            ref[x] = jnp.zeros((Y2, 128), F32)
        loop(0, X2, clear)

    def guard1(a):
        for x in (0, X1 - 1):
            L1[a, x] = jnp.zeros((Y1, 128), F32)

        def edge(x):
            L1[a, x, 0:8] = jnp.zeros((8, 128), F32)
            L1[a, x, 56:64] = jnp.zeros((8, 128), F32)
        loop(1, X1 - 1, edge)
    loop(0, 5, guard1)

    def guard2(a):
        for x in (0, 1, 2, 3, 20, 21, 22, 23):
            L2[a, x] = jnp.zeros((Y2, 128), F32)

        def edge(x):
            L2[a, x, 0:8] = jnp.zeros((8, 128), F32)
            L2[a, x, 40:48] = jnp.zeros((8, 128), F32)
        loop(4, 20, edge)
    loop(0, 5, guard2)

    lane80, row80 = lanes(80), rows_of(80)
    y_in = ((gy * 64 + row80 - 8) >= 0) & ((gy * 64 + row80 - 8) < 256)
    M[0] = jnp.where(y_in, 1.0, 0.0)
    z_in = ((lane80 < 8) & (gz < 7)) | ((lane80 >= 120) & (gz > 0))
    M[1] = jnp.where(y_in & z_in, 1.0, 0.0)

    for copy in za:
        copy.wait_recv()
    zb = []
    for i, (dx, dy) in enumerate(PLANAR):
        ys, yd = y_range(dy, 8, 64)
        zb.append(send(zr0.at[1, :, :, ys], zr0.at[1 - dx, :, :, yd], s_b0.at[i], r_b0.at[i], peer(dx, dy, 0)))
    started += za + zb
    for copy in first:
        copy.wait_recv()
        copy.wait_send()
    for copy in zb:
        copy.wait_recv()

    def x_in(x):
        return ((gx * 16 + x - 8) >= 0) & ((gx * 16 + x - 8) < 64)

    CH = 40
    lane = lanes(CH)
    at0, at127 = lane == 0, lane == 127

    def z_pair(t0, t1):
        r0, r1 = pltpu.roll(t0, 1, 1), pltpu.roll(t1, 1, 1)
        q0, q1 = pltpu.roll(t0, 127, 1), pltpu.roll(t1, 127, 1)
        return (
            jnp.where(at0, r1, r0) + jnp.where(at127, q1, q0),
            jnp.where(at0, r0, r1) + jnp.where(at127, q0, q1),
        )

    def around(ref, x, lo):
        t = [ref[k, x, lo : lo + CH] for k in range(2)]
        z = z_pair(*t)
        total = []
        for k in range(2):
            total.append(
                (ref[k, x - 1, lo : lo + CH] + ref[k, x + 1, lo : lo + CH])
                + (ref[k, x, lo - 1 : lo + CH - 1] + ref[k, x, lo + 1 : lo + CH + 1])
                + z[k]
            )
        return t, total

    def spread(x):
        p, n = lax.rem(x + 8, 16), (x + 8) // 16
        inside = x_in(x)
        for lo in (8, 8 + CH):
            r = pl.ds(lo - 8, CH)
            for k, ref in enumerate((E, L)):
                up = pltpu.roll(zr0[n, 1, k, r], lax.rem(256 - 8 * p, 128), 1)
                down = pltpu.roll(zr0[n, 0, k, r], lax.rem(248 - 8 * p, 128), 1)
                both = jnp.where(lane < 8, up, down)
                if k == 1:
                    ref[1, x, lo : lo + CH] = both
                    continue
                for t, v in ((0, ref[0, x, lo : lo + CH]), (1, both)):
                    m = jnp.where(inside, M[t, r], 0.0) > 0.5
                    v = jnp.where(m, v, 1.0)
                    E[t, x, lo : lo + CH] = v
                    R[t, x, lo : lo + CH] = 1.0 / v
    loop(1, 31, spread)

    def heights(x):
        for lo in (8, 8 + CH):
            e, es = around(E, x, lo)
            c, cs = around(R, x, lo)
            for k in range(2):
                t = (e[k] + es[k]) * (c[k] + cs[k])
                H[k, x, lo : lo + CH] = lax.rsqrt(lax.rsqrt(lax.rsqrt(t)))
    loop(2, 30, heights)

    def cells_of(v):
        return SCREENING + SEED_WEIGHT * jnp.where(v != 2.0, 1.0, 0.0)

    def row_pairs(slot, v):
        n = v.shape[0]
        tmp[slot, 0:n] = v
        return tmp[slot, pl.ds(0, n // 2, stride=2)] + tmp[slot, pl.ds(1, n // 2, stride=2)]

    lane64 = lanes(64)

    def coarse(i):
        x = 8 + 2 * i
        bufs[0, i] = row_pairs(0, cells_of(L[0, x, 16:80]) + cells_of(L[0, x + 1, 16:80]))
        wyb[i] = (
            H[0, x, pl.ds(16, 40, stride=2)] * H[0, x, pl.ds(15, 40, stride=2)]
            + H[0, x + 1, pl.ds(16, 40, stride=2)] * H[0, x + 1, pl.ds(15, 40, stride=2)]
        )
        total = None
        for k in range(2):
            h0, h1 = H[0, x + k, 16:80], H[1, x + k, 16:80]
            r0, r1 = pltpu.roll(h0, 1, 1), pltpu.roll(h1, 1, 1)
            v = h0 * jnp.where(lane64 == 0, r1, r0)
            beyond = pltpu.roll(h1, 1, 1) * pltpu.roll(h0, 2, 1)
            v = jnp.where(lane64 == 1, beyond, v)
            total = v if total is None else total + v
        bufs[1, i] = row_pairs(1, total)
    loop(0, 8, coarse)

    def coarse_x(i):
        x = 8 + 2 * i
        wx1[i] = row_pairs(2, H[0, x, 16:80] * H[0, x - 1, 16:80])
    loop(0, 9, coarse_x)

    wr, wc = rows_of(128), lanes(128)
    restrict = jnp.where(wc == 32 + wr // 2, 1.0, 0.0)
    even = jnp.where((wc == 32 + wr // 2) & (lax.rem(wr, 2) == 0), 1.0, 0.0)
    last = jnp.where((wr == 1) & (wc == 96), 1.0, 0.0)
    c1[...] = dot(bufs[0].reshape(256, 128), restrict).reshape(8, 32, 128)
    wx1[...] = dot(wx1[...].reshape(288, 128), restrict).reshape(9, 32, 128)
    wy1[:, 0:40] = dot(wyb[...].reshape(320, 128), restrict).reshape(8, 40, 128)
    wz1[...] = dot(bufs[1].reshape(256, 128), even + last).reshape(8, 32, 128)

    lane32 = lanes(32)
    own1 = (lane32 >= 32) & (lane32 < 96)

    def level1(i):
        wz = wz1[i]
        d = (
            c1[i] + (wx1[i] + wx1[i + 1]) + (wy1[i, 0:32] + wy1[i, 1:33])
            + (wz + pltpu.roll(wz, 127, 1))
        )
        D1[i] = jnp.where(own1, d, 0.0)
        L1[0, 8 + i, 16:48] = jnp.where(own1, 1.0 / jnp.where(own1, d, 1.0), 0.0)
        L1[1, 8 + i, 16:48] = wx1[i]
        L1[2, 8 + i, 16:48] = wy1[i, 0:32]
        L1[3, 8 + i, 16:48] = wz
    loop(0, 8, level1)

    lane16 = lanes(16)
    own2 = (lane16 >= 48) & (lane16 < 80)
    c2 = [row_pairs(0, c1[2 * i] + c1[2 * i + 1]) for i in range(4)]
    z2 = [row_pairs(1, wz1[2 * i] + wz1[2 * i + 1]) for i in range(4)]
    x2 = [row_pairs(2, wx1[2 * i]) for i in range(5)]
    y2 = [
        wy1[2 * i, pl.ds(0, 24, stride=2)] + wy1[2 * i + 1, pl.ds(0, 24, stride=2)] for i in range(4)
    ]
    c2 = dot(jnp.concatenate(c2, 0), restrict)
    x2 = dot(jnp.concatenate(x2, 0), restrict)
    y2 = dot(jnp.concatenate(y2, 0), restrict)
    z2 = dot(jnp.concatenate(z2, 0), even)
    for i in range(4):
        for k in range(3):
            tmp[k, 0:24] = y2[24 * i : 24 * i + 24]
        wz = z2[16 * i : 16 * i + 16]
        d = (
            c2[16 * i : 16 * i + 16]
            + (x2[16 * i : 16 * i + 16] + x2[16 * i + 16 : 16 * i + 32])
            + (tmp[0, 0:16] + tmp[0, 1:17]) + (wz + pltpu.roll(wz, 127, 1))
        )
        D2[i] = jnp.where(own2, d, 0.0)
        at = 4 + 4 * gx + i
        L2[0, at, 16:32] = jnp.where(own2, 1.0 / jnp.where(own2, d, 1.0), 0.0)
        L2[1, at, 16:32] = x2[16 * i : 16 * i + 16]
        L2[2, at, 16:32] = tmp[0, 0:16]
        L2[3, at, 16:32] = wz

    group32, group16 = lane32 // 8, lane16 // 8

    def pack_z(ref, a, base, planes, rows, lo, hi, group, dst):
        acc = jnp.zeros((rows, 128), F32)
        for p in range(planes):
            v = ref[a, base + p, 16 : 16 + rows]
            acc = jnp.where(group == p, pltpu.roll(v, (8 * p - lo) % 128, 1), acc)
            acc = jnp.where(group == 8 + p, pltpu.roll(v, (64 + 8 * p - hi) % 128, 1), acc)
        dst[a] = acc

    def unpack_z(ref, a, base, planes, rows, lo, hi, ln, src):
        below, above = src[0, a], src[1, a]
        for p in range(planes):
            v = ref[a, base + p, 16 : 16 + rows]
            v = jnp.where((ln >= lo - 8) & (ln < lo), pltpu.roll(below, (lo - 8 - 64 - 8 * p) % 128, 1), v)
            v = jnp.where((ln >= hi + 8) & (ln < hi + 16), pltpu.roll(above, (hi + 8 - 8 * p) % 128, 1), v)
            ref[a, base + p, 16 : 16 + rows] = v

    def pack1(a):
        pack_z(L1, a, 8, 8, 32, 32, 88, group32, zs1)

    def unpack1(a):
        unpack_z(L1, a, 8, 8, 32, 32, 88, lane32, zr1)

    def pack2(a):
        pack_z(L2, a, 4 + 4 * gx, 4, 16, 48, 72, group16, zs2)

    def unpack2(a):
        unpack_z(L2, a, 4 + 4 * gx, 4, 16, 48, 72, lane16, zr2)

    def send_z(zs, zr, which, n, ssem, rsem, slot):
        return [
            send(zs.at[pl.ds(which, n)], zr.at[s, pl.ds(which, n)], ssem.at[slot, s], rsem.at[slot, s],
                 peer(0, 0, 1 if s == 0 else -1))
            for s in range(2)
        ]

    def send_1(which, n, slot):
        copies = []
        for i, (dx, dy) in enumerate(PLANAR):
            ys, yd = y_range(dy, 16, 32)
            xs, xd = x_range(dx, 8, 8, 7)
            copies.append(send(L1.at[pl.ds(which, n), xs, ys], L1.at[pl.ds(which, n), xd, yd],
                               s_b1.at[slot, i], r_b1.at[slot, i], peer(dx, dy, 0)))
        return copies

    def send_2(which, n, slot):
        copies = []
        planes = pl.ds(4 + 4 * gx, 4)
        for i, (dx, dy) in enumerate(COLUMN):
            ys, yd = y_range(dy, 16, 16)
            copies.append(send(L2.at[pl.ds(which, n), planes, ys], L2.at[pl.ds(which, n), planes, yd],
                               s_b2.at[slot, i], r_b2.at[slot, i], peer(dx, dy, 0)))
        return copies

    loop(0, 4, pack1)
    a1 = send_z(zs1, zr1, 0, 4, s_a1, r_a1, 0)
    loop(0, 4, pack2)
    a2 = send_z(zs2, zr2, 0, 4, s_a2, r_a2, 0)

    def diagonal(x):
        inside = x_in(x)
        for lo in (8, 8 + CH):
            h, hs = around(H, x, lo)
            r = pl.ds(lo - 8, CH)
            for k in range(2):
                m = jnp.where(inside, M[k, r], 0.0)
                lab = L[k, x, lo : lo + CH]
                d = cells_of(lab) + h[k] * hs[k]
                hi = m * h[k] / d
                c = jnp.where(lab == 1.0, SEED_WEIGHT * hi, 0.0)
                C[k, x, lo : lo + CH] = c
                Q[k, x, lo : lo + CH] = hi * h[k]
                u = c * (1.0 / THETA)
                UA[k, x, lo : lo + CH] = u
                DU[k, x, lo : lo + CH] = u
                if k == 0:
                    DH[x, lo - 8 : lo - 8 + CH] = d / h[k]
    loop(3, 29, diagonal)

    for copy in a1 + a2:
        copy.wait_recv()
    loop(0, 4, unpack1)
    b1 = send_1(0, 4, 0)
    loop(0, 4, unpack2)
    b2 = send_2(0, 4, 0)
    started += a1 + a2 + b1 + b2

    def smooth(src, dst, lo_x, hi_x, alpha, beta, keep=True):
        def body(x):
            for lo in (8, 8 + CH):
                u, us = around(src, x, lo)
                for k in range(2):
                    s = slice(lo, lo + CH)
                    g = beta * (C[k, x, s] - u[k] + Q[k, x, s] * us[k])
                    d = g if alpha is None else alpha * DU[k, x, s] + g
                    if keep:
                        DU[k, x, s] = d
                    dst[k, x, s] = u[k] + d
        loop(lo_x, hi_x, body)

    fine = factors(SMOOTH_STEPS)
    smooth(UA, UB, 4, 28, *fine[0])
    smooth(UB, UA, 5, 27, *fine[1], keep=False)

    def own_sum(ref, x):
        t0, t1 = ref[0, x, 16:80], ref[1, x, 16:80]
        low = jnp.where(lane64 == 0, pltpu.roll(t1, 1, 1), pltpu.roll(t0, 1, 1))
        high = jnp.where(lane64 == 127, pltpu.roll(t1, 127, 1), pltpu.roll(t0, 127, 1))
        return t0, (
            (ref[0, x - 1, 16:80] + ref[0, x + 1, 16:80])
            + (ref[0, x, 15:79] + ref[0, x, 17:81]) + (low + high)
        )

    def residual(i):
        total = None
        for k in range(2):
            x = 8 + 2 * i + k
            u, us = own_sum(UA, x)
            r = DH[x, 8:72] * (C[0, x, 16:80] - u + Q[0, x, 16:80] * us)
            total = r if total is None else total + r
        bufs[0, i] = row_pairs(0, total)
    loop(0, 8, residual)
    L1[4, 8:16, 16:48] = dot(bufs[0].reshape(256, 128), restrict).reshape(8, 32, 128)
    pack1(4)
    a1 = send_z(zs1, zr1, 4, 1, s_a1, r_a1, 1)

    def prepare(ref, inv, a, x_lo, x_hi, rows, inside):
        def body(x):
            i = jnp.where(inside(x), ref[0, x, 8 : 8 + rows], 0.0)
            inv[x, 8 : 8 + rows] = i
            a[0, x] = i * ref[1, x, 8 : 8 + rows]
            a[1, x] = i * ref[1, x + 1, 8 : 8 + rows]
            a[2, x] = i * ref[2, x, 8 : 8 + rows]
            a[3, x] = i * ref[2, x, 9 : 9 + rows]
            a[4, x] = i * ref[3, x, 8 : 8 + rows]
            a[5, x] = i * pltpu.roll(ref[3, x, 8 : 8 + rows], 127, 1)
        loop(x_lo, x_hi, body)

    def apply(c, a, e, x, rows):
        v = e[x, 8 : 8 + rows]
        return v, (
            (c[x] - v)
            + (a[0, x] * e[x - 1, 8 : 8 + rows] + a[1, x] * e[x + 1, 8 : 8 + rows])
            + (a[2, x] * e[x, 7 : 7 + rows] + a[3, x] * e[x, 9 : 9 + rows])
            + (a[4, x] * pltpu.roll(v, 1, 1) + a[5, x] * pltpu.roll(v, 127, 1))
        )

    def begin(c, e, d, x_lo, x_hi, rows):
        def body(x):
            u = c[x] * (1.0 / THETA)
            e[x, 8 : 8 + rows] = u
            d[x, 0:rows] = u
        loop(x_lo, x_hi, body)

    def relax(c, a, e, new, d, x_lo, x_hi, rows, alpha, beta):
        def body(x):
            v, g = apply(c, a, e, x, rows)
            step = beta * g if alpha is None else alpha * d[x, 0:rows] + beta * g
            d[x, 0:rows] = step
            new[x, 8 : 8 + rows] = v + step
        loop(x_lo, x_hi, body)

    lane48, row48 = lanes(48), rows_of(48)
    yz1 = (
        (gy * 32 + row48 - 8 >= 0) & (gy * 32 + row48 - 8 < 128)
        & (gz * 64 + lane48 - 32 >= 0) & (gz * 64 + lane48 - 32 < 512)
    )

    def inside1(x):
        ok = ((gx * 8 + x - 8) >= 0) & ((gx * 8 + x - 8) < 32)
        return jnp.where(ok, jnp.where(yz1, 1.0, 0.0), 0.0) > 0.5

    row32 = rows_of(32)
    yz2 = (
        (gy * 16 + row32 - 8 >= 0) & (gy * 16 + row32 - 8 < 64)
        & (gz * 32 + lane32 - 48 >= 0) & (gz * 32 + lane32 - 48 < 256)
    )

    for copy in a1:
        copy.wait_recv()
    unpack1(4)
    r1 = send_1(4, 1, 1)
    started += a1 + r1
    for copy in b1:
        copy.wait_recv()
    prepare(L1, I1, A1, 1, X1 - 1, 48, inside1)
    for copy in r1:
        copy.wait_recv()

    def scale1(x):
        C1[x] = I1[x, 8:56] * L1[4, x, 8:56]
    loop(1, X1 - 1, scale1)
    begin(C1, ea1, d1, 1, X1 - 1, 48)
    relax(C1, A1, ea1, eb1, d1, 2, X1 - 2, 48, *fine[0])
    relax(C1, A1, eb1, ea1, d1, 3, X1 - 3, 48, *fine[1])

    def residual1(i):
        total = None
        for k in range(2):
            x = 8 + 2 * i + k
            _, g = apply(C1, A1, ea1, x, 48)
            r = D1[2 * i + k] * g[8:40]
            total = r if total is None else total + r
        bufs[1, i, 0:16] = row_pairs(1, total)
    loop(0, 4, residual1)
    r2 = dot(jnp.concatenate([bufs[1, i, 0:16] for i in range(4)], 0), restrict)
    for i in range(4):
        L2[4, 4 + 4 * gx + i, 16:32] = r2[16 * i : 16 * i + 16]
    pack2(4)
    a2 = send_z(zs2, zr2, 4, 1, s_a2, r_a2, 1)
    for copy in b2:
        copy.wait_recv()
    prepare(L2, I2, A2, 4, 20, 32, lambda x: yz2)
    for copy in a2:
        copy.wait_recv()
    unpack2(4)
    r2 = send_2(4, 1, 1)
    started += a2 + r2
    for copy in r2:
        copy.wait_recv()

    def scale2(x):
        C2[x] = I2[x, 8:40] * L2[4, x, 8:40]
    loop(4, 20, scale2)
    begin(C2, ea2, d2, 4, 20, 32)
    pair = (ea2, eb2)
    for n, f in enumerate(factors(COARSE_STEPS)):
        relax(C2, A2, pair[n % 2], pair[1 - n % 2], d2, 4, 20, 32, *f)
    e2 = pair[(COARSE_STEPS - 1) % 2]

    widen = jnp.where(wr == 32 + wc // 2, 1.0, 0.0)

    def up1(i):
        v = dot(e2[4 * gx + i, 8:40], widen)
        pro[0, pl.ds(0, 32, stride=2)] = v
        pro[0, pl.ds(1, 32, stride=2)] = v
        for k in range(2):
            ea1[2 * i + k, 8:56] = ea1[2 * i + k, 8:56] + pro[0, 8:56]
    loop(1, 11, up1)
    relax(C1, A1, ea1, eb1, d1, 3, X1 - 3, 48, None, 1.0 / THETA)
    relax(C1, A1, eb1, ea1, d1, 4, X1 - 4, 48, *fine[0])
    relax(C1, A1, ea1, eb1, d1, 5, X1 - 5, 48, *fine[1])

    beyond = jnp.where(
        ((wc < 8) & (wr == 96 + wc // 2)) | ((wc >= 120) & (wr == 28 + (wc - 120) // 2)), 1.0, 0.0
    )

    def up0(i):
        e = eb1[4 + i, 8:56]
        for k, w in enumerate((widen, beyond)):
            v = dot(e, w)
            pro[k, pl.ds(0, 48, stride=2)] = v
            pro[k, pl.ds(1, 48, stride=2)] = v
        for n in range(2):
            for k in range(2):
                x = 2 * i + n
                UA[k, x, 8:88] = UA[k, x, 8:88] + H[k, x, 8:88] * pro[k, 8:88]
    loop(2, 14, up0)
    smooth(UA, UB, 6, 26, None, 1.0 / THETA)
    smooth(UB, UA, 7, 25, *fine[0])

    def finish(x):
        u, us = own_sum(UA, 8 + x)
        alpha, beta = fine[1]
        d = alpha * DU[0, 8 + x, 16:80] + beta * (C[0, 8 + x, 16:80] - u + Q[0, 8 + x, 16:80] * us)
        out[x] = (u + d) / H[0, 8 + x, 16:80]
    loop(0, 16, finish)

    for copy in started:
        copy.wait_send()


def shards(image, labels):
    def level0():
        return pltpu.VMEM((2, X0, Y0, 128), F32)

    def vmem(*shape):
        return pltpu.VMEM(shape, F32)

    def sems(*shape):
        return pltpu.SemaphoreType.DMA(shape)

    scratch = [level0() for _ in range(9)] + [
        vmem(X0, 80, 128), vmem(2, 80, 128),
        vmem(2, 2, 64, 128), vmem(3, 2, 2, 80, 128), vmem(3, 64, 128), vmem(2, 8, 32, 128), vmem(8, 40, 128),
        vmem(8, 32, 128), vmem(9, 32, 128), vmem(8, 48, 128), vmem(8, 32, 128), vmem(8, 32, 128),
        vmem(5, X1, Y1, 128), vmem(5, 32, 128), vmem(2, 5, 32, 128), vmem(6, X1, 48, 128),
        vmem(X1, Y1, 128), vmem(X1, 48, 128), vmem(X1, Y1, 128), vmem(X1, Y1, 128), vmem(X1, Y1, 128),
        vmem(5, X2, Y2, 128), vmem(5, 16, 128), vmem(2, 5, 16, 128), vmem(6, X2, 32, 128),
        vmem(X2, Y2, 128), vmem(X2, 32, 128), vmem(X2, Y2, 128), vmem(X2, Y2, 128), vmem(X2, Y2, 128),
        vmem(4, 16, 128), vmem(2, 96, 128),
        sems(8), sems(8), sems(8), sems(8), sems(2), sems(2), sems(8), sems(8),
        sems(2, 2), sems(2, 2), sems(2, 8), sems(2, 8), sems(2, 2), sems(2, 2), sems(2, 11), sems(2, 11),
    ]
    return pl.pallas_call(
        kernel,
        out_shape=jax.ShapeDtypeStruct(image.shape, F32),
        in_specs=[pl.BlockSpec(memory_space=pltpu.VMEM)] * 2,
        out_specs=pl.BlockSpec(memory_space=pltpu.VMEM),
        scratch_shapes=scratch,
        compiler_params=pltpu.CompilerParams(
            collective_id=0, has_side_effects=True, vmem_limit_bytes=56 * 1024 * 1024
        ),
    )(image, labels)


def solution(mesh):
    placed = (P("gx", "gy", "gz"), P("gx", "gy", "gz"))
    return jax.shard_map(
        shards, mesh=mesh, in_specs=placed, out_specs=P("gx", "gy", "gz"), check_vma=False
    )
```

time: 905 us -> 111 us (0.12); the launches traced: 889 us -> 111 us
  blocking collectives: 239 us -> 0 us
  local copies, waits for them, and re-layouts: 198 us -> 1.89 us
  starting transfers between devices: 189 us -> 0 us
  other arithmetic: 172 us -> 0 us
  Pallas kernels: 0 us -> 109 us
  waiting for transfers between devices: 88.5 us -> 0 us
    all_gather x16 -> x0, blocking collectives: 239 us -> none  [the longest x1 17 us: shards(): lax.all_gather(faces_mid[4], 'gx', axis=0, tiled=True)]
    ppermute x76 -> x0, starting transfers between devices: 189 us -> none  [the longest x38 138 us: extended(): lax.ppermute(lax.slice_in_dim(block, block.shape[dim] - width, None, axis...]
    slice x65 -> x0, local copies, waits for them, and re-layouts: 109 us -> none  [the longest x14 46.5 us: coarsen_face_weights(): picked = lax.slice_in_dim(arr, start, arr.shape[axis_dim], 2, axis_dim)]
    pallas_call x0 -> x1, Pallas kernels: none -> 109 us  [shards(): pl.pallas_call(kernel, out_shape=jax.ShapeDtypeStruct(image.shape, F32),...]
    ppermute x76 -> x0, waiting for transfers between devices: 88.5 us -> none  [the longest x38 86 us: extended(): lax.ppermute(lax.slice_in_dim(block, 0, width, axis=dim), axis, backward)]
    add x20 -> x0, other arithmetic: 75.9 us -> none  [the longest x15 63.8 us: chebyshev(): field = field + update]
    ppermute x26 -> x0, local copies, waits for them, and re-layouts: 46 us -> none  [the longest x13 23.5 us: extended(): lax.ppermute(lax.slice_in_dim(block, 0, width, axis=dim), axis, backward)]
    reduce_sum x36 -> x0, other arithmetic: 40.5 us -> none  [pair_sum(): arr.reshape(shape[:axis_dim] + (shape[axis_dim] // 2, 2) + shape[axis_dim...]
  transfers between devices with their start and end apart: 76 -> 0, of which waited for: 37 -> 0; matrix products, arithmetic and copies ran while one was open for 11% -> 0% of each run, Pallas kernels for 0% -> 0%
where the time goes in v1:
time: 111 us
  Pallas kernels  109 us (98%)
  local copies, waits for them, and re-layouts  1.89 us (2%)
    pallas_call x1, Pallas kernels, shards(): pl.pallas_call(kernel, out_shape=jax.ShapeDtypeStruct(image.shape, F32),...  109 us

profile of v1, /device:TPU:0, one launch (start us, length us, event | category | flops | bytes accessed | tf_op | source)
XLA Modules:
  0.0 110.7 jit_solution(10389680992735121310)
XLA Ops:
  0.0 108.8 %shard_map.28 = f32[16,64,128]{2,1,0:T(8,128)} custom-call(f32[16,64,128]{2,1,0:T(8,128)} %image.1, s32[16,64,128]{2,1,0:T(8,128)} %labels.1), custom_call_target="tpu_custom_call" | custom-call | tf_op jit(solution)/shard_map/pallas_call | solution.py:618
  108.8 1.9 %copy.4 = f32[16,64,128]{2,1,0:T(8,128)} copy(f32[16,64,128]{2,1,0:T(8,128)} %shard_map.28) | data formatting | bytes 1048576

commit v2 on v1

--- a/solution.py
+++ b/solution.py
@@ -47,12 +47,12 @@
 
 def kernel(
     image, labels, out,
-    E, L, R, H, UA, UB, DU, C, Q, DH, M,
+    E, L, EM, R, H, UA, UB, DU, C, Q, DH, M,
     zs0, zr0, tmp, bufs, wyb, c1, wx1, wy1, wz1, D1,
-    L1, zs1, zr1, A1, I1, C1, ea1, eb1, d1,
-    L2, zs2, zr2, A2, I2, C2, ea2, eb2, d2, D2, pro,
+    L1, LP, zs1, zr1, zc1, A1, I1, C1, ea1, eb1, d1,
+    L2, LQ, zs2, zr2, zc2, A2, I2, C2, ea2, eb2, d2, D2, pro,
     s_e, r_e, s_l, r_l, s_z0, r_z0, s_b0, r_b0,
-    s_a1, r_a1, s_b1, r_b1, s_a2, r_a2, s_b2, r_b2,
+    s_a1, r_a1, s_b1, r_b1, s_c1, r_c1, s_a2, r_a2, s_b2, r_b2, s_c2, r_c2,
 ):
     gx, gy, gz = (lax.axis_index(a) for a in ("gx", "gy", "gz"))
     barrier = pltpu.get_barrier_semaphore()
@@ -81,9 +81,22 @@
             return carry
         lax.fori_loop(lo, hi, step, 0)
 
+    def grouped(lo, hi, n, work):
+        def step(i, carry):
+            stores = []
+            for j in range(n):
+                stores += work(lo + n * i + j)
+            for ref, index, value in stores:
+                ref[index] = value
+            return carry
+        lax.fori_loop(0, (hi - lo) // n, step, 0)
+        for j in range(lo + (hi - lo) // n * n, hi):
+            for ref, index, value in work(j):
+                ref[index] = value
+
     def own(x):
-        E[0, 8 + x, 16:80] = jnp.exp(image[x] * (1.0 / HEAT_CONSTANT))
-        L[0, 8 + x, 16:80] = labels[x].astype(F32)
+        E[8 + x, 16:80] = jnp.exp(image[x] * (1.0 / HEAT_CONSTANT))
+        L[8 + x, 16:80] = labels[x].astype(F32)
     loop(0, 16, own)
     pl.semaphore_wait(barrier, len(partners))
 
@@ -101,20 +114,22 @@
             return pl.ds(start + count - 8, 8), pl.ds(start - 8, 8)
         return pl.ds(start, 8), pl.ds(start + count, 8)
 
-    first = []
-    for i, (dx, dy) in enumerate(PLANAR):
-        ys, yd = y_range(dy, 16, 64)
-        xs, xd = x_range(dx, 8, 16, 7)
-        first.append(send(E.at[0, xs, ys], E.at[0, xd, yd], s_e.at[i], r_e.at[i], peer(dx, dy, 0)))
-        xs, xd = x_range(dx, 8, 16, 5)
-        first.append(send(L.at[0, xs, ys], L.at[0, xd, yd], s_l.at[i], r_l.at[i], peer(dx, dy, 0)))
+    def send_own(ref, width, ssem, rsem):
+        copies = []
+        for i, (dx, dy) in enumerate(PLANAR):
+            ys, yd = y_range(dy, 16, 64)
+            xs, xd = x_range(dx, 8, 16, width)
+            copies.append(send(ref.at[xs, ys], ref.at[xd, yd], ssem.at[i], rsem.at[i], peer(dx, dy, 0)))
+        return copies
+
+    own_e = send_own(E, 7, s_e, r_e)
 
     group64 = lanes(64) // 8
 
     def pack(p, carry):
         result = []
         for k, ref in enumerate((E, L)):
-            v = ref[0, 8 + p, 16:80]
+            v = ref[8 + p, 16:80]
             low = pltpu.roll(v, lax.rem(8 * p, 128), 1)
             high = pltpu.roll(v, lax.rem(8 * p + 8, 128), 1)
             result.append(jnp.where(group64 == p, low, carry[2 * k]))
@@ -124,12 +139,26 @@
     zero64 = jnp.zeros((64, 128), F32)
     packed = lax.fori_loop(0, 16, pack, (zero64,) * 4)
     for k in range(2):
-        zs0[1, k] = packed[2 * k]
-        zs0[0, k] = packed[2 * k + 1]
+        zs0[k, 1] = packed[2 * k]
+        zs0[k, 0] = packed[2 * k + 1]
     za = [
-        send(zs0.at[s], zr0.at[1, s, :, pl.ds(8, 64)], s_z0.at[s], r_z0.at[s], peer(0, 0, 1 if s == 0 else -1))
-        for s in range(2)
+        [
+            send(zs0.at[k, s], zr0.at[k, 1, s, pl.ds(8, 64)], s_z0.at[k, s], r_z0.at[k, s],
+                 peer(0, 0, 1 if s == 0 else -1))
+            for s in range(2)
+        ]
+        for k in range(2)
     ]
+
+    def forward(k):
+        for copy in za[k]:
+            copy.wait_recv()
+        copies = []
+        for i, (dx, dy) in enumerate(PLANAR):
+            ys, yd = y_range(dy, 8, 64)
+            copies.append(send(zr0.at[k, 1, :, ys], zr0.at[k, 1 - dx, :, yd],
+                               s_b0.at[k, i], r_b0.at[k, i], peer(dx, dy, 0)))
+        return copies
 
     for ref in (ea1, eb1, d1):
         def clear(x, ref=ref):
@@ -166,18 +195,14 @@
     z_in = ((lane80 < 8) & (gz < 7)) | ((lane80 >= 120) & (gz > 0))
     M[1] = jnp.where(y_in & z_in, 1.0, 0.0)
 
-    for copy in za:
-        copy.wait_recv()
-    zb = []
+    zb_e = forward(0)
+    own_l = send_own(L, 5, s_l, r_l)
+    zb_l = forward(1)
+    started += za[0] + za[1] + own_e + own_l + zb_e + zb_l
     for i, (dx, dy) in enumerate(PLANAR):
-        ys, yd = y_range(dy, 8, 64)
-        zb.append(send(zr0.at[1, :, :, ys], zr0.at[1 - dx, :, :, yd], s_b0.at[i], r_b0.at[i], peer(dx, dy, 0)))
-    started += za + zb
-    for copy in first:
-        copy.wait_recv()
-        copy.wait_send()
-    for copy in zb:
-        copy.wait_recv()
+        if dx == 0:
+            own_e[i].wait_recv()
+            zb_e[i].wait_recv()
 
     def x_in(x):
         return ((gx * 16 + x - 8) >= 0) & ((gx * 16 + x - 8) < 64)
@@ -206,33 +231,39 @@
             )
         return t, total
 
+    def ends(k, x, r):
+        p, n = lax.rem(x + 8, 16), (x + 8) // 16
+        up = pltpu.roll(zr0[k, n, 1, r], lax.rem(256 - 8 * p, 128), 1)
+        down = pltpu.roll(zr0[k, n, 0, r], lax.rem(248 - 8 * p, 128), 1)
+        return jnp.where(lane < 8, up, down)
+
     def spread(x):
-        p, n = lax.rem(x + 8, 16), (x + 8) // 16
         inside = x_in(x)
         for lo in (8, 8 + CH):
             r = pl.ds(lo - 8, CH)
-            for k, ref in enumerate((E, L)):
-                up = pltpu.roll(zr0[n, 1, k, r], lax.rem(256 - 8 * p, 128), 1)
-                down = pltpu.roll(zr0[n, 0, k, r], lax.rem(248 - 8 * p, 128), 1)
-                both = jnp.where(lane < 8, up, down)
-                if k == 1:
-                    ref[1, x, lo : lo + CH] = both
-                    continue
-                for t, v in ((0, ref[0, x, lo : lo + CH]), (1, both)):
-                    m = jnp.where(inside, M[t, r], 0.0) > 0.5
-                    v = jnp.where(m, v, 1.0)
-                    E[t, x, lo : lo + CH] = v
-                    R[t, x, lo : lo + CH] = 1.0 / v
-    loop(1, 31, spread)
+            for t, v in ((0, E[x, lo : lo + CH]), (1, ends(0, x, r))):
+                m = jnp.where(inside, M[t, r], 0.0) > 0.5
+                v = jnp.where(m, v, 1.0)
+                EM[t, x, lo : lo + CH] = v
+                R[t, x, lo : lo + CH] = 1.0 / v
+    loop(8, 24, spread)
 
     def heights(x):
         for lo in (8, 8 + CH):
-            e, es = around(E, x, lo)
+            e, es = around(EM, x, lo)
             c, cs = around(R, x, lo)
             for k in range(2):
                 t = (e[k] + es[k]) * (c[k] + cs[k])
                 H[k, x, lo : lo + CH] = lax.rsqrt(lax.rsqrt(lax.rsqrt(t)))
-    loop(2, 30, heights)
+    loop(9, 23, heights)
+    for i, (dx, dy) in enumerate(PLANAR):
+        if dx != 0:
+            own_e[i].wait_recv()
+            zb_e[i].wait_recv()
+    loop(6, 8, spread)
+    loop(24, 26, spread)
+    loop(7, 9, heights)
+    loop(23, 25, heights)
 
     def cells_of(v):
         return SCREENING + SEED_WEIGHT * jnp.where(v != 2.0, 1.0, 0.0)
@@ -246,7 +277,7 @@
 
     def coarse(i):
         x = 8 + 2 * i
-        bufs[0, i] = row_pairs(0, cells_of(L[0, x, 16:80]) + cells_of(L[0, x + 1, 16:80]))
+        bufs[0, i] = row_pairs(0, cells_of(L[x, 16:80]) + cells_of(L[x + 1, 16:80]))
         wyb[i] = (
             H[0, x, pl.ds(16, 40, stride=2)] * H[0, x, pl.ds(15, 40, stride=2)]
             + H[0, x + 1, pl.ds(16, 40, stride=2)] * H[0, x + 1, pl.ds(15, 40, stride=2)]
@@ -286,11 +317,25 @@
             + (wz + pltpu.roll(wz, 127, 1))
         )
         D1[i] = jnp.where(own1, d, 0.0)
-        L1[0, 8 + i, 16:48] = jnp.where(own1, 1.0 / jnp.where(own1, d, 1.0), 0.0)
-        L1[1, 8 + i, 16:48] = wx1[i]
-        L1[2, 8 + i, 16:48] = wy1[i, 0:32]
-        L1[3, 8 + i, 16:48] = wz
+        four = (jnp.where(own1, 1.0 / jnp.where(own1, d, 1.0), 0.0), wx1[i], wy1[i, 0:32], wz)
+        for a in range(4):
+            L1[a, 8 + i, 16:48] = four[a]
+        for a in range(2):
+            LP[a, 8 + i, 16:48] = jnp.where(
+                lane32 < 64, pltpu.roll(four[2 * a], 96, 1), pltpu.roll(four[2 * a + 1], 32, 1)
+            )
     loop(0, 8, level1)
+
+    def send_1(src, which, width, ssem, rsem):
+        copies = []
+        for i, (dx, dy) in enumerate(PLANAR):
+            ys, yd = y_range(dy, 16, 32)
+            xs, xd = x_range(dx, 8, 8, 7)
+            copies.append(send(src.at[pl.ds(which, width), xs, ys], src.at[pl.ds(which, width), xd, yd],
+                               ssem.at[i], rsem.at[i], peer(dx, dy, 0)))
+        return copies
+
+    b1 = send_1(LP, 0, 2, s_b1.at[0], r_b1.at[0])
 
     lane16 = lanes(16)
     own2 = (lane16 >= 48) & (lane16 < 80)
@@ -330,25 +375,41 @@
             acc = jnp.where(group == 8 + p, pltpu.roll(v, (64 + 8 * p - hi) % 128, 1), acc)
         dst[a] = acc
 
-    def unpack_z(ref, a, base, planes, rows, lo, hi, ln, src):
-        below, above = src[0, a], src[1, a]
-        for p in range(planes):
-            v = ref[a, base + p, 16 : 16 + rows]
-            v = jnp.where((ln >= lo - 8) & (ln < lo), pltpu.roll(below, (lo - 8 - 64 - 8 * p) % 128, 1), v)
-            v = jnp.where((ln >= hi + 8) & (ln < hi + 16), pltpu.roll(above, (hi + 8 - 8 * p) % 128, 1), v)
-            ref[a, base + p, 16 : 16 + rows] = v
+    def joined(zr, zc, a, slot, rows, ln):
+        zc[a, slot, 8 : 8 + rows] = jnp.where(ln < 64, zr[1, a], zr[0, a])
+
+    def extended(base, ends, p, ln, lo, hi):
+        down = pltpu.roll(ends, lax.rem(256 + lo - 8 - 64 - 8 * p, 128), 1)
+        up = pltpu.roll(ends, lax.rem(256 + hi + 8 - 8 * p, 128), 1)
+        v = jnp.where((ln >= lo) & (ln < hi + 8), base, 0.0)
+        v = jnp.where((ln >= lo - 8) & (ln < lo), down, v)
+        return jnp.where((ln >= hi + 8) & (ln < hi + 16), up, v)
 
     def pack1(a):
         pack_z(L1, a, 8, 8, 32, 32, 88, group32, zs1)
 
-    def unpack1(a):
-        unpack_z(L1, a, 8, 8, 32, 32, 88, lane32, zr1)
+    def join1(a):
+        joined(zr1, zc1, a, 1, 32, lane32)
+
+    def extended1(a, x, base):
+        return extended(base, zc1[a, x // 8], lax.rem(x, 8), lane48, 32, 88)
 
     def pack2(a):
         pack_z(L2, a, 4 + 4 * gx, 4, 16, 48, 72, group16, zs2)
 
-    def unpack2(a):
-        unpack_z(L2, a, 4 + 4 * gx, 4, 16, 48, 72, lane16, zr2)
+    def join2(a):
+        joined(zr2, zc2, a, gx, 16, lane16)
+
+    def pack_own2(a):
+        acc = jnp.zeros((16, 128), F32)
+        for p in range(4):
+            v = pltpu.roll(L2[a, 4 + 4 * gx + p, 16:32], (32 * p - 48) % 128, 1)
+            acc = jnp.where(lane16 // 32 == p, v, acc)
+        LQ[a, gx, 8:24] = acc
+
+    def extended2(a, slot, p):
+        base = pltpu.roll(LQ[a, slot], (48 - 32 * p) % 128, 1)
+        return extended(base, zc2[a, slot], p, lane32, 48, 72)
 
     def send_z(zs, zr, which, n, ssem, rsem, slot):
         return [
@@ -357,28 +418,36 @@
             for s in range(2)
         ]
 
-    def send_1(which, n, slot):
+    def send_c1(which, n, slot):
         copies = []
         for i, (dx, dy) in enumerate(PLANAR):
-            ys, yd = y_range(dy, 16, 32)
-            xs, xd = x_range(dx, 8, 8, 7)
-            copies.append(send(L1.at[pl.ds(which, n), xs, ys], L1.at[pl.ds(which, n), xd, yd],
-                               s_b1.at[slot, i], r_b1.at[slot, i], peer(dx, dy, 0)))
+            ys, yd = y_range(dy, 8, 32)
+            copies.append(send(zc1.at[pl.ds(which, n), 1, ys], zc1.at[pl.ds(which, n), 1 - dx, yd],
+                               s_c1.at[slot, i], r_c1.at[slot, i], peer(dx, dy, 0)))
         return copies
 
-    def send_2(which, n, slot):
+    def send_2(ref, which, n, ssem, rsem):
         copies = []
-        planes = pl.ds(4 + 4 * gx, 4)
         for i, (dx, dy) in enumerate(COLUMN):
-            ys, yd = y_range(dy, 16, 16)
-            copies.append(send(L2.at[pl.ds(which, n), planes, ys], L2.at[pl.ds(which, n), planes, yd],
-                               s_b2.at[slot, i], r_b2.at[slot, i], peer(dx, dy, 0)))
+            ys, yd = y_range(dy, 8, 16)
+            copies.append(send(ref.at[pl.ds(which, n), gx, ys], ref.at[pl.ds(which, n), gx, yd],
+                               ssem.at[i], rsem.at[i], peer(dx, dy, 0)))
         return copies
 
+    lane48, row48 = lanes(48), rows_of(48)
     loop(0, 4, pack1)
     a1 = send_z(zs1, zr1, 0, 4, s_a1, r_a1, 0)
     loop(0, 4, pack2)
     a2 = send_z(zs2, zr2, 0, 4, s_a2, r_a2, 0)
+    loop(0, 4, pack_own2)
+    loop(1, 6, spread)
+    loop(26, 31, spread)
+    loop(2, 7, heights)
+    loop(25, 30, heights)
+    for copy in a1:
+        copy.wait_recv()
+    loop(0, 4, join1)
+    c1s = send_c1(0, 4, 0)
 
     def diagonal(x):
         inside = x_in(x)
@@ -387,7 +456,7 @@
             r = pl.ds(lo - 8, CH)
             for k in range(2):
                 m = jnp.where(inside, M[k, r], 0.0)
-                lab = L[k, x, lo : lo + CH]
+                lab = L[x, lo : lo + CH] if k == 0 else ends(1, x, r)
                 d = cells_of(lab) + h[k] * hs[k]
                 hi = m * h[k] / d
                 c = jnp.where(lab == 1.0, SEED_WEIGHT * hi, 0.0)
@@ -398,15 +467,10 @@
                 DU[k, x, lo : lo + CH] = u
                 if k == 0:
                     DH[x, lo - 8 : lo - 8 + CH] = d / h[k]
+    for copy in own_l + zb_l:
+        copy.wait_recv()
     loop(3, 29, diagonal)
-
-    for copy in a1 + a2:
-        copy.wait_recv()
-    loop(0, 4, unpack1)
-    b1 = send_1(0, 4, 0)
-    loop(0, 4, unpack2)
-    b2 = send_2(0, 4, 0)
-    started += a1 + a2 + b1 + b2
+    started += a1 + a2 + b1 + c1s
 
     def smooth(src, dst, lo_x, hi_x, alpha, beta, keep=True):
         def body(x):
@@ -446,6 +510,7 @@
     L1[4, 8:16, 16:48] = dot(bufs[0].reshape(256, 128), restrict).reshape(8, 32, 128)
     pack1(4)
     a1 = send_z(zs1, zr1, 4, 1, s_a1, r_a1, 1)
+    r1 = send_1(L1, 4, 1, s_b1.at[1], r_b1.at[1])
 
     def prepare(ref, inv, a, x_lo, x_hi, rows, inside):
         def body(x):
@@ -479,11 +544,12 @@
         def body(x):
             v, g = apply(c, a, e, x, rows)
             step = beta * g if alpha is None else alpha * d[x, 0:rows] + beta * g
-            d[x, 0:rows] = step
-            new[x, 8 : 8 + rows] = v + step
-        loop(x_lo, x_hi, body)
-
-    lane48, row48 = lanes(48), rows_of(48)
+            return [
+                (d, (x, slice(0, rows)), step),
+                (new, (x, slice(8, 8 + rows)), v + step),
+            ]
+        grouped(x_lo, x_hi, 4 if rows == 32 else 2, body)
+
     yz1 = (
         (gy * 32 + row48 - 8 >= 0) & (gy * 32 + row48 - 8 < 128)
         & (gz * 64 + lane48 - 32 >= 0) & (gz * 64 + lane48 - 32 < 512)
@@ -499,19 +565,29 @@
         & (gz * 32 + lane32 - 48 >= 0) & (gz * 32 + lane32 - 48 < 256)
     )
 
+    def assemble1(x):
+        for a in range(4):
+            base = pltpu.roll(LP[a // 2, x, 8:56], 32 if a % 2 == 0 else 96, 1)
+            L1[a, x, 8:56] = extended1(a, x, base)
     for copy in a1:
         copy.wait_recv()
-    unpack1(4)
-    r1 = send_1(4, 1, 1)
-    started += a1 + r1
-    for copy in b1:
-        copy.wait_recv()
+    join1(4)
+    c1r = send_c1(4, 1, 1)
+    for copy in a2:
+        copy.wait_recv()
+    loop(0, 4, join2)
+    b2 = send_2(LQ, 0, 4, s_b2.at[0], r_b2.at[0])
+    c2 = send_2(zc2, 0, 4, s_c2.at[0], r_c2.at[0])
+    started += a1 + r1 + c1r + b2 + c2
+    for copy in b1 + c1s:
+        copy.wait_recv()
+    loop(1, X1 - 1, assemble1)
     prepare(L1, I1, A1, 1, X1 - 1, 48, inside1)
-    for copy in r1:
+    for copy in r1 + c1r:
         copy.wait_recv()
 
     def scale1(x):
-        C1[x] = I1[x, 8:56] * L1[4, x, 8:56]
+        C1[x] = I1[x, 8:56] * extended1(4, x, L1[4, x, 8:56])
     loop(1, X1 - 1, scale1)
     begin(C1, ea1, d1, 1, X1 - 1, 48)
     relax(C1, A1, ea1, eb1, d1, 2, X1 - 2, 48, *fine[0])
@@ -531,20 +607,30 @@
         L2[4, 4 + 4 * gx + i, 16:32] = r2[16 * i : 16 * i + 16]
     pack2(4)
     a2 = send_z(zs2, zr2, 4, 1, s_a2, r_a2, 1)
-    for copy in b2:
-        copy.wait_recv()
+    pack_own2(4)
+    r2 = send_2(LQ, 4, 1, s_b2.at[1], r_b2.at[1])
+    for copy in b2 + c2:
+        copy.wait_recv()
+
+    def assemble2(slot):
+        for a in range(4):
+            for p in range(4):
+                L2[a, 4 + 4 * slot + p, 8:40] = extended2(a, slot, p)
+    for copy in a2:
+        copy.wait_recv()
+    join2(4)
+    c2r = send_2(zc2, 4, 1, s_c2.at[1], r_c2.at[1])
+    loop(0, 4, assemble2)
     prepare(L2, I2, A2, 4, 20, 32, lambda x: yz2)
-    for copy in a2:
-        copy.wait_recv()
-    unpack2(4)
-    r2 = send_2(4, 1, 1)
-    started += a2 + r2
-    for copy in r2:
-        copy.wait_recv()
-
-    def scale2(x):
-        C2[x] = I2[x, 8:40] * L2[4, x, 8:40]
-    loop(4, 20, scale2)
+    started += a2 + r2 + c2r
+    for copy in r2 + c2r:
+        copy.wait_recv()
+
+    def scale2(slot):
+        for p in range(4):
+            x = 4 + 4 * slot + p
+            C2[x] = I2[x, 8:40] * extended2(4, slot, p)
+    loop(0, 4, scale2)
     begin(C2, ea2, d2, 4, 20, 32)
     pair = (ea2, eb2)
     for n, f in enumerate(factors(COARSE_STEPS)):
@@ -603,17 +689,18 @@
     def sems(*shape):
         return pltpu.SemaphoreType.DMA(shape)
 
-    scratch = [level0() for _ in range(9)] + [
+    scratch = [vmem(X0, Y0, 128), vmem(X0, Y0, 128)] + [level0() for _ in range(8)] + [
         vmem(X0, 80, 128), vmem(2, 80, 128),
-        vmem(2, 2, 64, 128), vmem(3, 2, 2, 80, 128), vmem(3, 64, 128), vmem(2, 8, 32, 128), vmem(8, 40, 128),
+        vmem(2, 2, 64, 128), vmem(2, 3, 2, 80, 128), vmem(3, 64, 128), vmem(2, 8, 32, 128), vmem(8, 40, 128),
         vmem(8, 32, 128), vmem(9, 32, 128), vmem(8, 48, 128), vmem(8, 32, 128), vmem(8, 32, 128),
-        vmem(5, X1, Y1, 128), vmem(5, 32, 128), vmem(2, 5, 32, 128), vmem(6, X1, 48, 128),
+        vmem(5, X1, Y1, 128), vmem(2, X1, Y1, 128), vmem(5, 32, 128), vmem(2, 5, 32, 128), vmem(5, 3, 48, 128), vmem(6, X1, 48, 128),
         vmem(X1, Y1, 128), vmem(X1, 48, 128), vmem(X1, Y1, 128), vmem(X1, Y1, 128), vmem(X1, Y1, 128),
-        vmem(5, X2, Y2, 128), vmem(5, 16, 128), vmem(2, 5, 16, 128), vmem(6, X2, 32, 128),
+        vmem(5, X2, Y2, 128), vmem(5, 4, 32, 128), vmem(5, 16, 128), vmem(2, 5, 16, 128), vmem(5, 4, 32, 128), vmem(6, X2, 32, 128),
         vmem(X2, Y2, 128), vmem(X2, 32, 128), vmem(X2, Y2, 128), vmem(X2, Y2, 128), vmem(X2, Y2, 128),
         vmem(4, 16, 128), vmem(2, 96, 128),
-        sems(8), sems(8), sems(8), sems(8), sems(2), sems(2), sems(8), sems(8),
-        sems(2, 2), sems(2, 2), sems(2, 8), sems(2, 8), sems(2, 2), sems(2, 2), sems(2, 11), sems(2, 11),
+        sems(8), sems(8), sems(8), sems(8), sems(2, 2), sems(2, 2), sems(2, 8), sems(2, 8),
+        sems(2, 2), sems(2, 2), sems(2, 8), sems(2, 8), sems(2, 8), sems(2, 8),
+        sems(2, 2), sems(2, 2), sems(2, 11), sems(2, 11), sems(2, 11), sems(2, 11),
     ]
     return pl.pallas_call(
         kernel,

time: 111 us -> 83.3 us (0.75)
  Pallas kernels: 109 us -> 81.2 us
    pallas_call x1, Pallas kernels: 109 us -> 81.2 us  [shards(): pl.pallas_call(kernel, out_shape=jax.ShapeDtypeStruct(image.shape, F32),...]
where the time goes in v2:
time: 83.3 us; the launch traced here: 83.1 us
  Pallas kernels  81.2 us (97%)
  local copies, waits for them, and re-layouts  1.89 us (2%)
    pallas_call x1, Pallas kernels, shards(): pl.pallas_call(kernel, out_shape=jax.ShapeDtypeStruct(image.shape, F32),...  81.2 us
    unnamed x1, local copies, waits for them, and re-layouts  1.89 us

profile of v2, /device:TPU:0, one launch (start us, length us, event | category | flops | bytes accessed | tf_op | source)
XLA Modules:
  0.0 83.1 jit_solution(891037327202221028)
XLA Ops:
  0.0 81.2 %shard_map.28 = f32[16,64,128]{2,1,0:T(8,128)} custom-call(f32[16,64,128]{2,1,0:T(8,128)} %image.1, s32[16,64,128]{2,1,0:T(8,128)} %labels.1), custom_call_target="tpu_custom_call" | custom-call | tf_op jit(solution)/shard_map/pallas_call | solution.py:705
  81.2 1.9 %copy.4 = f32[16,64,128]{2,1,0:T(8,128)} copy(f32[16,64,128]{2,1,0:T(8,128)} %shard_map.28) | data formatting | bytes 1048576

commit v3 on v2

--- a/solution.py
+++ b/solution.py
@@ -46,13 +46,15 @@
 
 
 def kernel(
+    image_hbm, labels_hbm, out_hbm,
     image, labels, out,
     E, L, EM, R, H, UA, UB, DU, C, Q, DH, M,
     zs0, zr0, tmp, bufs, wyb, c1, wx1, wy1, wz1, D1,
     L1, LP, zs1, zr1, zc1, A1, I1, C1, ea1, eb1, d1,
-    L2, LQ, zs2, zr2, zc2, A2, I2, C2, ea2, eb2, d2, D2, pro,
+    L2, LQ, zs2, zr2, zc2, A2, I2, C2, ea2, eb2, d2, D2, pro, PR,
     s_e, r_e, s_l, r_l, s_z0, r_z0, s_b0, r_b0,
     s_a1, r_a1, s_b1, r_b1, s_c1, r_c1, s_a2, r_a2, s_b2, r_b2, s_c2, r_c2,
+    s_in, s_out,
 ):
     gx, gy, gz = (lax.axis_index(a) for a in ("gx", "gy", "gz"))
     barrier = pltpu.get_barrier_semaphore()
@@ -60,6 +62,13 @@
     for p in partners:
         pl.semaphore_signal(barrier, inc=1, device_id=peer(*p), device_id_type=MESH)
 
+    loads = [
+        pltpu.make_async_copy(image_hbm, image, s_in.at[0]),
+        pltpu.make_async_copy(labels_hbm, labels, s_in.at[1]),
+    ]
+    for copy in loads:
+        copy.start()
+
     def lanes(rows):
         return lax.broadcasted_iota(jnp.int32, (rows, 128), 1)
 
@@ -81,22 +90,10 @@
             return carry
         lax.fori_loop(lo, hi, step, 0)
 
-    def grouped(lo, hi, n, work):
-        def step(i, carry):
-            stores = []
-            for j in range(n):
-                stores += work(lo + n * i + j)
-            for ref, index, value in stores:
-                ref[index] = value
-            return carry
-        lax.fori_loop(0, (hi - lo) // n, step, 0)
-        for j in range(lo + (hi - lo) // n * n, hi):
-            for ref, index, value in work(j):
-                ref[index] = value
+    loads[0].wait()
 
     def own(x):
         E[8 + x, 16:80] = jnp.exp(image[x] * (1.0 / HEAT_CONSTANT))
-        L[8 + x, 16:80] = labels[x].astype(F32)
     loop(0, 16, own)
     pl.semaphore_wait(barrier, len(partners))
 
@@ -123,6 +120,11 @@
         return copies
 
     own_e = send_own(E, 7, s_e, r_e)
+    loads[1].wait()
+
+    def own_labels(x):
+        L[8 + x, 16:80] = labels[x].astype(F32)
+    loop(0, 16, own_labels)
 
     group64 = lanes(64) // 8
 
@@ -207,7 +209,24 @@
     def x_in(x):
         return ((gx * 16 + x - 8) >= 0) & ((gx * 16 + x - 8) < 64)
 
-    CH = 40
+    CH, GROUP, CHC = 16, 4, 16
+
+    def sweep(lo_x, hi_x, work, n=GROUP):
+        def step(x, n):
+            for lo in range(8, 88, CH):
+                stores = []
+                for j in range(n):
+                    stores += work(x + j, lo)
+                for ref, index, value in stores:
+                    ref[index] = value
+
+        def body(i, carry):
+            step(lo_x + n * i, n)
+            return carry
+        lax.fori_loop(0, (hi_x - lo_x) // n, body, 0)
+        if (hi_x - lo_x) % n:
+            step(hi_x - (hi_x - lo_x) % n, (hi_x - lo_x) % n)
+
     lane = lanes(CH)
     at0, at127 = lane == 0, lane == 127
 
@@ -237,33 +256,37 @@
         down = pltpu.roll(zr0[k, n, 0, r], lax.rem(248 - 8 * p, 128), 1)
         return jnp.where(lane < 8, up, down)
 
-    def spread(x):
+    def spread(x, lo):
         inside = x_in(x)
-        for lo in (8, 8 + CH):
-            r = pl.ds(lo - 8, CH)
-            for t, v in ((0, E[x, lo : lo + CH]), (1, ends(0, x, r))):
-                m = jnp.where(inside, M[t, r], 0.0) > 0.5
-                v = jnp.where(m, v, 1.0)
-                EM[t, x, lo : lo + CH] = v
-                R[t, x, lo : lo + CH] = 1.0 / v
-    loop(8, 24, spread)
-
-    def heights(x):
-        for lo in (8, 8 + CH):
-            e, es = around(EM, x, lo)
-            c, cs = around(R, x, lo)
-            for k in range(2):
-                t = (e[k] + es[k]) * (c[k] + cs[k])
-                H[k, x, lo : lo + CH] = lax.rsqrt(lax.rsqrt(lax.rsqrt(t)))
-    loop(9, 23, heights)
+        r = pl.ds(lo - 8, CH)
+        s = slice(lo, lo + CH)
+        stores = []
+        for t, v in ((0, E[x, s]), (1, ends(0, x, r))):
+            m = jnp.where(inside, M[t, r], 0.0) > 0.5
+            v = jnp.where(m, v, 1.0)
+            stores += [(EM, (t, x, s), v), (R, (t, x, s), 1.0 / v)]
+        return stores
+
+    sweep(8, 24, spread)
+
+    def heights(x, lo):
+        e, es = around(EM, x, lo)
+        c, cs = around(R, x, lo)
+        stores = []
+        for k in range(2):
+            t = (e[k] + es[k]) * (c[k] + cs[k])
+            stores.append((H, (k, x, slice(lo, lo + CH)), lax.rsqrt(lax.rsqrt(lax.rsqrt(t)))))
+        return stores
+
+    sweep(9, 23, heights)
     for i, (dx, dy) in enumerate(PLANAR):
         if dx != 0:
             own_e[i].wait_recv()
             zb_e[i].wait_recv()
-    loop(6, 8, spread)
-    loop(24, 26, spread)
-    loop(7, 9, heights)
-    loop(23, 25, heights)
+    sweep(6, 8, spread)
+    sweep(24, 26, spread)
+    sweep(7, 9, heights)
+    sweep(23, 25, heights)
 
     def cells_of(v):
         return SCREENING + SEED_WEIGHT * jnp.where(v != 2.0, 1.0, 0.0)
@@ -440,72 +463,81 @@
     loop(0, 4, pack2)
     a2 = send_z(zs2, zr2, 0, 4, s_a2, r_a2, 0)
     loop(0, 4, pack_own2)
-    loop(1, 6, spread)
-    loop(26, 31, spread)
-    loop(2, 7, heights)
-    loop(25, 30, heights)
+    sweep(1, 6, spread)
+    sweep(26, 31, spread)
+    sweep(2, 7, heights)
+    sweep(25, 30, heights)
     for copy in a1:
         copy.wait_recv()
     loop(0, 4, join1)
     c1s = send_c1(0, 4, 0)
 
-    def diagonal(x):
+    def diagonal(x, lo):
         inside = x_in(x)
-        for lo in (8, 8 + CH):
-            h, hs = around(H, x, lo)
-            r = pl.ds(lo - 8, CH)
-            for k in range(2):
-                m = jnp.where(inside, M[k, r], 0.0)
-                lab = L[x, lo : lo + CH] if k == 0 else ends(1, x, r)
-                d = cells_of(lab) + h[k] * hs[k]
-                hi = m * h[k] / d
-                c = jnp.where(lab == 1.0, SEED_WEIGHT * hi, 0.0)
-                C[k, x, lo : lo + CH] = c
-                Q[k, x, lo : lo + CH] = hi * h[k]
-                u = c * (1.0 / THETA)
-                UA[k, x, lo : lo + CH] = u
-                DU[k, x, lo : lo + CH] = u
-                if k == 0:
-                    DH[x, lo - 8 : lo - 8 + CH] = d / h[k]
+        h, hs = around(H, x, lo)
+        r = pl.ds(lo - 8, CH)
+        s = slice(lo, lo + CH)
+        stores = []
+        for k in range(2):
+            m = jnp.where(inside, M[k, r], 0.0)
+            lab = L[x, s] if k == 0 else ends(1, x, r)
+            d = cells_of(lab) + h[k] * hs[k]
+            hi = m * h[k] / d
+            c = jnp.where(lab == 1.0, SEED_WEIGHT * hi, 0.0)
+            u = c * (1.0 / THETA)
+            stores += [
+                (C, (k, x, s), c), (Q, (k, x, s), hi * h[k]), (UA, (k, x, s), u), (DU, (k, x, s), u)
+            ]
+            if k == 0:
+                stores.append((DH, (x, r), d / h[k]))
+        return stores
+
     for copy in own_l + zb_l:
         copy.wait_recv()
-    loop(3, 29, diagonal)
+    sweep(3, 29, diagonal)
     started += a1 + a2 + b1 + c1s
 
     def smooth(src, dst, lo_x, hi_x, alpha, beta, keep=True):
-        def body(x):
-            for lo in (8, 8 + CH):
-                u, us = around(src, x, lo)
-                for k in range(2):
-                    s = slice(lo, lo + CH)
-                    g = beta * (C[k, x, s] - u[k] + Q[k, x, s] * us[k])
-                    d = g if alpha is None else alpha * DU[k, x, s] + g
-                    if keep:
-                        DU[k, x, s] = d
-                    dst[k, x, s] = u[k] + d
-        loop(lo_x, hi_x, body)
+        def work(x, lo):
+            u, us = around(src, x, lo)
+            s = slice(lo, lo + CH)
+            stores = []
+            for k in range(2):
+                g = beta * (C[k, x, s] - u[k] + Q[k, x, s] * us[k])
+                d = g if alpha is None else alpha * DU[k, x, s] + g
+                if keep:
+                    stores.append((DU, (k, x, s), d))
+                stores.append((dst, (k, x, s), u[k] + d))
+            return stores
+        sweep(lo_x, hi_x, work)
 
     fine = factors(SMOOTH_STEPS)
     smooth(UA, UB, 4, 28, *fine[0])
     smooth(UB, UA, 5, 27, *fine[1], keep=False)
 
-    def own_sum(ref, x):
-        t0, t1 = ref[0, x, 16:80], ref[1, x, 16:80]
-        low = jnp.where(lane64 == 0, pltpu.roll(t1, 1, 1), pltpu.roll(t0, 1, 1))
-        high = jnp.where(lane64 == 127, pltpu.roll(t1, 127, 1), pltpu.roll(t0, 127, 1))
+    lane_ch = lanes(CH)
+
+    def own_sum(ref, x, lo):
+        t0, t1 = ref[0, x, lo : lo + CH], ref[1, x, lo : lo + CH]
+        low = jnp.where(lane_ch == 0, pltpu.roll(t1, 1, 1), pltpu.roll(t0, 1, 1))
+        high = jnp.where(lane_ch == 127, pltpu.roll(t1, 127, 1), pltpu.roll(t0, 127, 1))
         return t0, (
-            (ref[0, x - 1, 16:80] + ref[0, x + 1, 16:80])
-            + (ref[0, x, 15:79] + ref[0, x, 17:81]) + (low + high)
+            (ref[0, x - 1, lo : lo + CH] + ref[0, x + 1, lo : lo + CH])
+            + (ref[0, x, lo - 1 : lo + CH - 1] + ref[0, x, lo + 1 : lo + CH + 1]) + (low + high)
         )
 
     def residual(i):
-        total = None
-        for k in range(2):
-            x = 8 + 2 * i + k
-            u, us = own_sum(UA, x)
-            r = DH[x, 8:72] * (C[0, x, 16:80] - u + Q[0, x, 16:80] * us)
-            total = r if total is None else total + r
-        bufs[0, i] = row_pairs(0, total)
+        x = 8 + 2 * i
+        for lo in range(16, 80, CH):
+            total = None
+            for k in range(2):
+                u, us = own_sum(UA, x + k, lo)
+                r = DH[x + k, lo - 8 : lo - 8 + CH] * (
+                    C[0, x + k, lo : lo + CH] - u + Q[0, x + k, lo : lo + CH] * us
+                )
+                total = r if total is None else total + r
+            tmp[0, lo - 16 : lo - 16 + CH] = total
+        bufs[0, i] = tmp[0, pl.ds(0, 32, stride=2)] + tmp[0, pl.ds(1, 32, stride=2)]
     loop(0, 8, residual)
     L1[4, 8:16, 16:48] = dot(bufs[0].reshape(256, 128), restrict).reshape(8, 32, 128)
     pack1(4)
@@ -524,13 +556,14 @@
             a[5, x] = i * pltpu.roll(ref[3, x, 8 : 8 + rows], 127, 1)
         loop(x_lo, x_hi, body)
 
-    def apply(c, a, e, x, rows):
-        v = e[x, 8 : 8 + rows]
+    def apply(c, a, e, x, lo, n):
+        r, s = slice(lo - 8, lo - 8 + n), slice(lo, lo + n)
+        v = e[x, s]
         return v, (
-            (c[x] - v)
-            + (a[0, x] * e[x - 1, 8 : 8 + rows] + a[1, x] * e[x + 1, 8 : 8 + rows])
-            + (a[2, x] * e[x, 7 : 7 + rows] + a[3, x] * e[x, 9 : 9 + rows])
-            + (a[4, x] * pltpu.roll(v, 1, 1) + a[5, x] * pltpu.roll(v, 127, 1))
+            (c[x, r] - v)
+            + (a[0, x, r] * e[x - 1, s] + a[1, x, r] * e[x + 1, s])
+            + (a[2, x, r] * e[x, lo - 1 : lo - 1 + n] + a[3, x, r] * e[x, lo + 1 : lo + 1 + n])
+            + (a[4, x, r] * pltpu.roll(v, 1, 1) + a[5, x, r] * pltpu.roll(v, 127, 1))
         )
 
     def begin(c, e, d, x_lo, x_hi, rows):
@@ -541,14 +574,25 @@
         loop(x_lo, x_hi, body)
 
     def relax(c, a, e, new, d, x_lo, x_hi, rows, alpha, beta):
-        def body(x):
-            v, g = apply(c, a, e, x, rows)
-            step = beta * g if alpha is None else alpha * d[x, 0:rows] + beta * g
-            return [
-                (d, (x, slice(0, rows)), step),
-                (new, (x, slice(8, 8 + rows)), v + step),
-            ]
-        grouped(x_lo, x_hi, 4 if rows == 32 else 2, body)
+        n = 2 if rows == 48 else 4
+
+        def step(x, n):
+            for lo in range(8, 8 + rows, CHC):
+                values = []
+                for j in range(n):
+                    v, g = apply(c, a, e, x + j, lo, CHC)
+                    r = slice(lo - 8, lo - 8 + CHC)
+                    move = beta * g if alpha is None else alpha * d[x + j, r] + beta * g
+                    values += [(d, (x + j, r), move), (new, (x + j, slice(lo, lo + CHC)), v + move)]
+                for ref, index, value in values:
+                    ref[index] = value
+
+        def body(i, carry):
+            step(x_lo + n * i, n)
+            return carry
+        lax.fori_loop(0, (x_hi - x_lo) // n, body, 0)
+        if (x_hi - x_lo) % n:
+            step(x_hi - (x_hi - x_lo) % n, (x_hi - x_lo) % n)
 
     yz1 = (
         (gy * 32 + row48 - 8 >= 0) & (gy * 32 + row48 - 8 < 128)
@@ -597,8 +641,8 @@
         total = None
         for k in range(2):
             x = 8 + 2 * i + k
-            _, g = apply(C1, A1, ea1, x, 48)
-            r = D1[2 * i + k] * g[8:40]
+            _, g = apply(C1, A1, ea1, x, 16, 32)
+            r = D1[2 * i + k] * g
             total = r if total is None else total + r
         bufs[1, i, 0:16] = row_pairs(1, total)
     loop(0, 4, residual1)
@@ -639,13 +683,23 @@
 
     widen = jnp.where(wr == 32 + wc // 2, 1.0, 0.0)
 
+    PR[0, 0:10, 0:32] = dot(
+        e2[pl.ds(4 * gx + 1, 10), 8:40].reshape(320, 128), widen
+    ).reshape(10, 32, 128)
+
     def up1(i):
-        v = dot(e2[4 * gx + i, 8:40], widen)
-        pro[0, pl.ds(0, 32, stride=2)] = v
-        pro[0, pl.ds(1, 32, stride=2)] = v
-        for k in range(2):
-            ea1[2 * i + k, 8:56] = ea1[2 * i + k, 8:56] + pro[0, 8:56]
-    loop(1, 11, up1)
+        for j in range(2):
+            v = PR[0, 2 * i + j, 0:32]
+            pro[j, pl.ds(0, 32, stride=2)] = v
+            pro[j, pl.ds(1, 32, stride=2)] = v
+        values = []
+        for j in range(2):
+            for k in range(2):
+                x = 2 + 4 * i + 2 * j + k
+                values.append((x, ea1[x, 8:56] + pro[j, 8:56]))
+        for x, value in values:
+            ea1[x, 8:56] = value
+    loop(0, 5, up1)
     relax(C1, A1, ea1, eb1, d1, 3, X1 - 3, 48, None, 1.0 / THETA)
     relax(C1, A1, eb1, ea1, d1, 4, X1 - 4, 48, *fine[0])
     relax(C1, A1, ea1, eb1, d1, 5, X1 - 5, 48, *fine[1])
@@ -654,26 +708,52 @@
         ((wc < 8) & (wr == 96 + wc // 2)) | ((wc >= 120) & (wr == 28 + (wc - 120) // 2)), 1.0, 0.0
     )
 
+    both = jnp.concatenate([widen, beyond], 1)
+    wide = dot(eb1[6:18, 8:56].reshape(576, 128), both)
+    for k in range(2):
+        PR[k] = wide[:, 128 * k : 128 * k + 128].reshape(12, 48, 128)
+
     def up0(i):
-        e = eb1[4 + i, 8:56]
-        for k, w in enumerate((widen, beyond)):
-            v = dot(e, w)
-            pro[k, pl.ds(0, 48, stride=2)] = v
-            pro[k, pl.ds(1, 48, stride=2)] = v
-        for n in range(2):
+        for j in range(2):
             for k in range(2):
-                x = 2 * i + n
-                UA[k, x, 8:88] = UA[k, x, 8:88] + H[k, x, 8:88] * pro[k, 8:88]
-    loop(2, 14, up0)
+                v = PR[k, 2 * i + j]
+                pro[2 * j + k, pl.ds(0, 48, stride=2)] = v
+                pro[2 * j + k, pl.ds(1, 48, stride=2)] = v
+        for lo in range(8, 88, CH):
+            s = slice(lo, lo + CH)
+            values = []
+            for j in range(2):
+                for n in range(2):
+                    x = 4 + 4 * i + 2 * j + n
+                    for k in range(2):
+                        values.append(((k, x, s), UA[k, x, s] + H[k, x, s] * pro[2 * j + k, s]))
+            for index, value in values:
+                UA[index] = value
+    loop(0, 6, up0)
     smooth(UA, UB, 6, 26, None, 1.0 / THETA)
     smooth(UB, UA, 7, 25, *fine[0])
 
-    def finish(x):
-        u, us = own_sum(UA, 8 + x)
-        alpha, beta = fine[1]
-        d = alpha * DU[0, 8 + x, 16:80] + beta * (C[0, 8 + x, 16:80] - u + Q[0, 8 + x, 16:80] * us)
-        out[x] = (u + d) / H[0, 8 + x, 16:80]
-    loop(0, 16, finish)
+    alpha, beta = fine[1]
+
+    def finish(i):
+        for lo in range(16, 80, CH):
+            values = []
+            for k in range(2):
+                x = 8 + 2 * i + k
+                s = slice(lo, lo + CH)
+                u, us = own_sum(UA, x, lo)
+                d = alpha * DU[0, x, s] + beta * (C[0, x, s] - u + Q[0, x, s] * us)
+                values.append((u + d) / H[0, x, s])
+            for k in range(2):
+                out[2 * i + k, lo - 16 : lo - 16 + CH] = values[k]
+    stores = []
+    for part in range(4):
+        loop(2 * part, 2 * part + 2, finish)
+        planes = pl.ds(4 * part, 4)
+        stores.append(pltpu.make_async_copy(out.at[planes], out_hbm.at[planes], s_out.at[part]))
+        stores[-1].start()
+    for copy in stores:
+        copy.wait()
 
     for copy in started:
         copy.wait_send()
@@ -689,7 +769,8 @@
     def sems(*shape):
         return pltpu.SemaphoreType.DMA(shape)
 
-    scratch = [vmem(X0, Y0, 128), vmem(X0, Y0, 128)] + [level0() for _ in range(8)] + [
+    scratch = [vmem(16, 64, 128), pltpu.VMEM((16, 64, 128), jnp.int32), vmem(16, 64, 128)]
+    scratch += [vmem(X0, Y0, 128), vmem(X0, Y0, 128)] + [level0() for _ in range(8)] + [
         vmem(X0, 80, 128), vmem(2, 80, 128),
         vmem(2, 2, 64, 128), vmem(2, 3, 2, 80, 128), vmem(3, 64, 128), vmem(2, 8, 32, 128), vmem(8, 40, 128),
         vmem(8, 32, 128), vmem(9, 32, 128), vmem(8, 48, 128), vmem(8, 32, 128), vmem(8, 32, 128),
@@ -697,16 +778,17 @@
         vmem(X1, Y1, 128), vmem(X1, 48, 128), vmem(X1, Y1, 128), vmem(X1, Y1, 128), vmem(X1, Y1, 128),
         vmem(5, X2, Y2, 128), vmem(5, 4, 32, 128), vmem(5, 16, 128), vmem(2, 5, 16, 128), vmem(5, 4, 32, 128), vmem(6, X2, 32, 128),
         vmem(X2, Y2, 128), vmem(X2, 32, 128), vmem(X2, Y2, 128), vmem(X2, Y2, 128), vmem(X2, Y2, 128),
-        vmem(4, 16, 128), vmem(2, 96, 128),
+        vmem(4, 16, 128), vmem(4, 96, 128), vmem(2, 12, 48, 128),
         sems(8), sems(8), sems(8), sems(8), sems(2, 2), sems(2, 2), sems(2, 8), sems(2, 8),
         sems(2, 2), sems(2, 2), sems(2, 8), sems(2, 8), sems(2, 8), sems(2, 8),
         sems(2, 2), sems(2, 2), sems(2, 11), sems(2, 11), sems(2, 11), sems(2, 11),
+        sems(2), sems(4),
     ]
     return pl.pallas_call(
         kernel,
         out_shape=jax.ShapeDtypeStruct(image.shape, F32),
-        in_specs=[pl.BlockSpec(memory_space=pltpu.VMEM)] * 2,
-        out_specs=pl.BlockSpec(memory_space=pltpu.VMEM),
+        in_specs=[pl.BlockSpec(memory_space=pl.ANY)] * 2,
+        out_specs=pl.BlockSpec(memory_space=pl.ANY),
         scratch_shapes=scratch,
         compiler_params=pltpu.CompilerParams(
             collective_id=0, has_side_effects=True, vmem_limit_bytes=56 * 1024 * 1024

time: 83.3 us -> 68 us (0.82)
  Pallas kernels: 81.2 us -> 65.9 us
    pallas_call x1, Pallas kernels: 81.2 us -> 65.9 us  [shards(): pl.pallas_call(kernel, out_shape=jax.ShapeDtypeStruct(image.shape, F32),...]
where the time goes in v3:
time: 68 us; the launch traced here: 67.8 us
  Pallas kernels  65.9 us (97%)
  local copies, waits for them, and re-layouts  1.89 us (3%)
    pallas_call x1, Pallas kernels, shards(): pl.pallas_call(kernel, out_shape=jax.ShapeDtypeStruct(image.shape, F32),...  65.9 us
    unnamed x1, local copies, waits for them, and re-layouts  1.89 us

profile of v3, /device:TPU:0, one launch (start us, length us, event | category | flops | bytes accessed | tf_op | source)
XLA Modules:
  0.0 67.8 jit_solution(931769981983001833)
XLA Ops:
  0.0 65.9 %shard_map.28 = f32[16,64,128]{2,1,0:T(8,128)} custom-call(f32[16,64,128]{2,1,0:T(8,128)} %image_hbm.1, s32[16,64,128]{2,1,0:T(8,128)} %labels_hbm.1), custom_call_target="tpu_custom_call" | custom-call | tf_op jit(solution)/shard_map/pallas_call | solution.py:787
  65.9 1.9 %copy.4 = f32[16,64,128]{2,1,0:T(8,128)} copy(f32[16,64,128]{2,1,0:T(8,128)} %shard_map.28) | data formatting | bytes 1048576

commit v4 on v3

--- a/solution.py
+++ b/solution.py
@@ -54,7 +54,7 @@
     L2, LQ, zs2, zr2, zc2, A2, I2, C2, ea2, eb2, d2, D2, pro, PR,
     s_e, r_e, s_l, r_l, s_z0, r_z0, s_b0, r_b0,
     s_a1, r_a1, s_b1, r_b1, s_c1, r_c1, s_a2, r_a2, s_b2, r_b2, s_c2, r_c2,
-    s_in, s_out,
+    s_in, s_out, XU, s_u, r_u,
 ):
     gx, gy, gz = (lax.axis_index(a) for a in ("gx", "gy", "gz"))
     barrier = pltpu.get_barrier_semaphore()
@@ -119,7 +119,7 @@
             copies.append(send(ref.at[xs, ys], ref.at[xd, yd], ssem.at[i], rsem.at[i], peer(dx, dy, 0)))
         return copies
 
-    own_e = send_own(E, 7, s_e, r_e)
+    own_e = send_own(E, 5, s_e, r_e)
     loads[1].wait()
 
     def own_labels(x):
@@ -198,7 +198,7 @@
     M[1] = jnp.where(y_in & z_in, 1.0, 0.0)
 
     zb_e = forward(0)
-    own_l = send_own(L, 5, s_l, r_l)
+    own_l = send_own(L, 3, s_l, r_l)
     zb_l = forward(1)
     started += za[0] + za[1] + own_e + own_l + zb_e + zb_l
     for i, (dx, dy) in enumerate(PLANAR):
@@ -463,10 +463,10 @@
     loop(0, 4, pack2)
     a2 = send_z(zs2, zr2, 0, 4, s_a2, r_a2, 0)
     loop(0, 4, pack_own2)
-    sweep(1, 6, spread)
-    sweep(26, 31, spread)
-    sweep(2, 7, heights)
-    sweep(25, 30, heights)
+    sweep(3, 6, spread)
+    sweep(26, 29, spread)
+    sweep(4, 7, heights)
+    sweep(25, 28, heights)
     for copy in a1:
         copy.wait_recv()
     loop(0, 4, join1)
@@ -494,7 +494,7 @@
 
     for copy in own_l + zb_l:
         copy.wait_recv()
-    sweep(3, 29, diagonal)
+    sweep(5, 27, diagonal)
     started += a1 + a2 + b1 + c1s
 
     def smooth(src, dst, lo_x, hi_x, alpha, beta, keep=True):
@@ -512,8 +512,8 @@
         sweep(lo_x, hi_x, work)
 
     fine = factors(SMOOTH_STEPS)
-    smooth(UA, UB, 4, 28, *fine[0])
-    smooth(UB, UA, 5, 27, *fine[1], keep=False)
+    smooth(UA, UB, 6, 26, *fine[0])
+    smooth(UB, UA, 7, 25, *fine[1], keep=False)
 
     lane_ch = lanes(CH)
 
@@ -613,6 +613,9 @@
         for a in range(4):
             base = pltpu.roll(LP[a // 2, x, 8:56], 32 if a % 2 == 0 else 96, 1)
             L1[a, x, 8:56] = extended1(a, x, base)
+    for copy in b1 + c1s:
+        copy.wait_recv()
+    loop(1, X1 - 1, assemble1)
     for copy in a1:
         copy.wait_recv()
     join1(4)
@@ -622,10 +625,11 @@
     loop(0, 4, join2)
     b2 = send_2(LQ, 0, 4, s_b2.at[0], r_b2.at[0])
     c2 = send_2(zc2, 0, 4, s_c2.at[0], r_c2.at[0])
+    fu = [
+        send(UA.at[:, pl.ds(21, 3), pl.ds(8, 80)], XU.at[0], s_u.at[0], r_u.at[0], peer(1, 0, 0)),
+        send(UA.at[:, pl.ds(8, 3), pl.ds(8, 80)], XU.at[1], s_u.at[1], r_u.at[1], peer(-1, 0, 0)),
+    ]
     started += a1 + r1 + c1r + b2 + c2
-    for copy in b1 + c1s:
-        copy.wait_recv()
-    loop(1, X1 - 1, assemble1)
     prepare(L1, I1, A1, 1, X1 - 1, 48, inside1)
     for copy in r1 + c1r:
         copy.wait_recv()
@@ -660,11 +664,11 @@
         for a in range(4):
             for p in range(4):
                 L2[a, 4 + 4 * slot + p, 8:40] = extended2(a, slot, p)
+    loop(0, 4, assemble2)
     for copy in a2:
         copy.wait_recv()
     join2(4)
     c2r = send_2(zc2, 4, 1, s_c2.at[1], r_c2.at[1])
-    loop(0, 4, assemble2)
     prepare(L2, I2, A2, 4, 20, 32, lambda x: yz2)
     started += a2 + r2 + c2r
     for copy in r2 + c2r:
@@ -707,6 +711,17 @@
     beyond = jnp.where(
         ((wc < 8) & (wr == 96 + wc // 2)) | ((wc >= 120) & (wr == 28 + (wc - 120) // 2)), 1.0, 0.0
     )
+
+    for copy in fu:
+        copy.wait_recv()
+        copy.wait_send()
+
+    def beside(i):
+        for side, x in ((0, 5 + i), (1, 24 + i)):
+            scale = jnp.where(x_in(x), 1.0, 0.0)
+            for k in range(2):
+                UA[k, x, 8:88] = XU[side, k, i] * scale
+    loop(0, 3, beside)
 
     both = jnp.concatenate([widen, beyond], 1)
     wide = dot(eb1[6:18, 8:56].reshape(576, 128), both)
@@ -782,7 +797,7 @@
         sems(8), sems(8), sems(8), sems(8), sems(2, 2), sems(2, 2), sems(2, 8), sems(2, 8),
         sems(2, 2), sems(2, 2), sems(2, 8), sems(2, 8), sems(2, 8), sems(2, 8),
         sems(2, 2), sems(2, 2), sems(2, 11), sems(2, 11), sems(2, 11), sems(2, 11),
-        sems(2), sems(4),
+        sems(2), sems(4), vmem(2, 2, 3, 80, 128), sems(2), sems(2),
     ]
     return pl.pallas_call(
         kernel,

time: 68 us -> 66.8 us (0.982); the launches traced: 67.8 us -> 65.6 us
  Pallas kernels: 65.9 us -> 63.7 us
    pallas_call x1, Pallas kernels: 65.9 us -> 63.7 us  [shards(): pl.pallas_call(kernel, out_shape=jax.ShapeDtypeStruct(image.shape, F32),...]
where the time goes in v4:
time: 66.8 us; the launch traced here: 65.6 us
  Pallas kernels  63.7 us (95%)
  local copies, waits for them, and re-layouts  1.89 us (3%)
    pallas_call x1, Pallas kernels, shards(): pl.pallas_call(kernel, out_shape=jax.ShapeDtypeStruct(image.shape, F32),...  63.7 us
    unnamed x1, local copies, waits for them, and re-layouts  1.89 us

profile of v4, /device:TPU:0, one launch (start us, length us, event | category | flops | bytes accessed | tf_op | source)
XLA Modules:
  0.0 65.6 jit_solution(12267024715250614223)
XLA Ops:
  0.0 63.7 %shard_map.28 = f32[16,64,128]{2,1,0:T(8,128)} custom-call(f32[16,64,128]{2,1,0:T(8,128)} %image_hbm.1, s32[16,64,128]{2,1,0:T(8,128)} %labels_hbm.1), custom_call_target="tpu_custom_call" | custom-call | tf_op jit(solution)/shard_map/pallas_call | solution.py:802
  63.7 1.9 %copy.4 = f32[16,64,128]{2,1,0:T(8,128)} copy(f32[16,64,128]{2,1,0:T(8,128)} %shard_map.28) | data formatting | bytes 1048576

commit v5 on v4

--- a/solution.py
+++ b/solution.py
@@ -84,11 +84,11 @@
 
     started = []
 
-    def loop(lo, hi, body):
+    def loop(lo, hi, body, unroll=1):
         def step(i, carry):
             body(i)
             return carry
-        lax.fori_loop(lo, hi, step, 0)
+        lax.fori_loop(lo, hi, step, 0, unroll=unroll)
 
     loads[0].wait()
 
@@ -314,12 +314,12 @@
             v = jnp.where(lane64 == 1, beyond, v)
             total = v if total is None else total + v
         bufs[1, i] = row_pairs(1, total)
-    loop(0, 8, coarse)
+    loop(0, 8, coarse, 2)
 
     def coarse_x(i):
         x = 8 + 2 * i
         wx1[i] = row_pairs(2, H[0, x, 16:80] * H[0, x - 1, 16:80])
-    loop(0, 9, coarse_x)
+    loop(0, 9, coarse_x, 3)
 
     wr, wc = rows_of(128), lanes(128)
     restrict = jnp.where(wc == 32 + wr // 2, 1.0, 0.0)
@@ -458,7 +458,7 @@
         return copies
 
     lane48, row48 = lanes(48), rows_of(48)
-    loop(0, 4, pack1)
+    loop(0, 4, pack1, 2)
     a1 = send_z(zs1, zr1, 0, 4, s_a1, r_a1, 0)
     loop(0, 4, pack2)
     a2 = send_z(zs2, zr2, 0, 4, s_a2, r_a2, 0)
@@ -538,7 +538,7 @@
                 total = r if total is None else total + r
             tmp[0, lo - 16 : lo - 16 + CH] = total
         bufs[0, i] = tmp[0, pl.ds(0, 32, stride=2)] + tmp[0, pl.ds(1, 32, stride=2)]
-    loop(0, 8, residual)
+    loop(0, 8, residual, 2)
     L1[4, 8:16, 16:48] = dot(bufs[0].reshape(256, 128), restrict).reshape(8, 32, 128)
     pack1(4)
     a1 = send_z(zs1, zr1, 4, 1, s_a1, r_a1, 1)
@@ -554,7 +554,7 @@
             a[3, x] = i * ref[2, x, 9 : 9 + rows]
             a[4, x] = i * ref[3, x, 8 : 8 + rows]
             a[5, x] = i * pltpu.roll(ref[3, x, 8 : 8 + rows], 127, 1)
-        loop(x_lo, x_hi, body)
+        loop(x_lo, x_hi, body, 2)
 
     def apply(c, a, e, x, lo, n):
         r, s = slice(lo - 8, lo - 8 + n), slice(lo, lo + n)
@@ -571,7 +571,7 @@
             u = c[x] * (1.0 / THETA)
             e[x, 8 : 8 + rows] = u
             d[x, 0:rows] = u
-        loop(x_lo, x_hi, body)
+        loop(x_lo, x_hi, body, 2)
 
     def relax(c, a, e, new, d, x_lo, x_hi, rows, alpha, beta):
         n = 2 if rows == 48 else 4
@@ -615,7 +615,7 @@
             L1[a, x, 8:56] = extended1(a, x, base)
     for copy in b1 + c1s:
         copy.wait_recv()
-    loop(1, X1 - 1, assemble1)
+    loop(1, X1 - 1, assemble1, 2)
     for copy in a1:
         copy.wait_recv()
     join1(4)
@@ -636,7 +636,7 @@
 
     def scale1(x):
         C1[x] = I1[x, 8:56] * extended1(4, x, L1[4, x, 8:56])
-    loop(1, X1 - 1, scale1)
+    loop(1, X1 - 1, scale1, 2)
     begin(C1, ea1, d1, 1, X1 - 1, 48)
     relax(C1, A1, ea1, eb1, d1, 2, X1 - 2, 48, *fine[0])
     relax(C1, A1, eb1, ea1, d1, 3, X1 - 3, 48, *fine[1])

time: 66.8 us -> 66.1 us (0.990); the launches traced: 65.6 us -> 65.9 us
  no operation moved by 1% of the time
where the time goes in v5:
time: 66.1 us; the launch traced here: 65.9 us
  Pallas kernels  64 us (97%)
  local copies, waits for them, and re-layouts  1.89 us (3%)
    pallas_call x1, Pallas kernels, shards(): pl.pallas_call(kernel, out_shape=jax.ShapeDtypeStruct(image.shape, F32),...  64 us
    unnamed x1, local copies, waits for them, and re-layouts  1.89 us

profile of v5, /device:TPU:0, one launch (start us, length us, event | category | flops | bytes accessed | tf_op | source)
XLA Modules:
  0.0 65.9 jit_solution(3540816869630819249)
XLA Ops:
  0.0 64.0 %shard_map.28 = f32[16,64,128]{2,1,0:T(8,128)} custom-call(f32[16,64,128]{2,1,0:T(8,128)} %image_hbm.1, s32[16,64,128]{2,1,0:T(8,128)} %labels_hbm.1), custom_call_target="tpu_custom_call" | custom-call | tf_op jit(solution)/shard_map/pallas_call | solution.py:802
  64.0 1.9 %copy.4 = f32[16,64,128]{2,1,0:T(8,128)} copy(f32[16,64,128]{2,1,0:T(8,128)} %shard_map.28) | data formatting | bytes 1048576

commit v6 on v5

--- a/solution.py
+++ b/solution.py
@@ -94,7 +94,7 @@
 
     def own(x):
         E[8 + x, 16:80] = jnp.exp(image[x] * (1.0 / HEAT_CONSTANT))
-    loop(0, 16, own)
+    loop(0, 16, own, 2)
     pl.semaphore_wait(barrier, len(partners))
 
     def x_range(dx, start, count, width):
@@ -347,7 +347,7 @@
             LP[a, 8 + i, 16:48] = jnp.where(
                 lane32 < 64, pltpu.roll(four[2 * a], 96, 1), pltpu.roll(four[2 * a + 1], 32, 1)
             )
-    loop(0, 8, level1)
+    loop(0, 8, level1, 2)
 
     def send_1(src, which, width, ssem, rsem):
         copies = []
@@ -649,7 +649,7 @@
             r = D1[2 * i + k] * g
             total = r if total is None else total + r
         bufs[1, i, 0:16] = row_pairs(1, total)
-    loop(0, 4, residual1)
+    loop(0, 4, residual1, 2)
     r2 = dot(jnp.concatenate([bufs[1, i, 0:16] for i in range(4)], 0), restrict)
     for i in range(4):
         L2[4, 4 + 4 * gx + i, 16:32] = r2[16 * i : 16 * i + 16]
@@ -664,7 +664,7 @@
         for a in range(4):
             for p in range(4):
                 L2[a, 4 + 4 * slot + p, 8:40] = extended2(a, slot, p)
-    loop(0, 4, assemble2)
+    loop(0, 4, assemble2, 2)
     for copy in a2:
         copy.wait_recv()
     join2(4)
@@ -678,7 +678,7 @@
         for p in range(4):
             x = 4 + 4 * slot + p
             C2[x] = I2[x, 8:40] * extended2(4, slot, p)
-    loop(0, 4, scale2)
+    loop(0, 4, scale2, 2)
     begin(C2, ea2, d2, 4, 20, 32)
     pair = (ea2, eb2)
     for n, f in enumerate(factors(COARSE_STEPS)):
@@ -744,7 +744,7 @@
                         values.append(((k, x, s), UA[k, x, s] + H[k, x, s] * pro[2 * j + k, s]))
             for index, value in values:
                 UA[index] = value
-    loop(0, 6, up0)
+    loop(0, 6, up0, 2)
     smooth(UA, UB, 6, 26, None, 1.0 / THETA)
     smooth(UB, UA, 7, 25, *fine[0])
 

time: 66.1 us -> 65.2 us (0.986)
  Pallas kernels: 64 us -> 63.1 us
    pallas_call x1, Pallas kernels: 64 us -> 63.1 us  [shards(): pl.pallas_call(kernel, out_shape=jax.ShapeDtypeStruct(image.shape, F32),...]
where the time goes in v6:
time: 65.2 us; the launch traced here: 65 us
  Pallas kernels  63.1 us (97%)
  local copies, waits for them, and re-layouts  1.89 us (3%)
    pallas_call x1, Pallas kernels, shards(): pl.pallas_call(kernel, out_shape=jax.ShapeDtypeStruct(image.shape, F32),...  63.1 us
    unnamed x1, local copies, waits for them, and re-layouts  1.89 us

profile of v6, /device:TPU:0, one launch (start us, length us, event | category | flops | bytes accessed | tf_op | source)
XLA Modules:
  0.0 65.0 jit_solution(17734595034389448832)
XLA Ops:
  0.0 63.1 %shard_map.28 = f32[16,64,128]{2,1,0:T(8,128)} custom-call(f32[16,64,128]{2,1,0:T(8,128)} %image_hbm.1, s32[16,64,128]{2,1,0:T(8,128)} %labels_hbm.1), custom_call_target="tpu_custom_call" | custom-call | tf_op jit(solution)/shard_map/pallas_call | solution.py:802
  63.1 1.9 %copy.4 = f32[16,64,128]{2,1,0:T(8,128)} copy(f32[16,64,128]{2,1,0:T(8,128)} %shard_map.28) | data formatting | bytes 1048576
